TPU v7x, 32 devices: a whole 2x2x4 slice. The times are simulated.
32 devices in a mesh: dp: 8 (over y, x, core), mp: 4 (over z).
Axes of the slice: x: 2, y: 2, z: 4, core: 2. Of those that a mesh axis runs over, the one named last changes fastest.
Arguments:
- video: bfloat16 [8, 8, 784, 768], P('mp', 'dp'), may hold values from -6 to 6
- patch_width: int32 [8], P('dp'), may hold values from 196 to 784, as said below
- temporal_gain: float32 [768], replicated, may hold values from 0.25 to 1.75
- temporal_shift: float32 [768], replicated, may hold values from -1.75 to 1.75
- temporal_qkv: bfloat16 [768, 2304], replicated, may hold values from -0.21875 to 0.21875
- temporal_qv_bias: float32 [1536], replicated, may hold values from -1.75 to 1.75
- temporal_proj: bfloat16 [768, 768], replicated, may hold values from -0.625 to 0.625
- temporal_proj_bias: float32 [768], replicated, may hold values from -1.75 to 1.75
- spatial_gain: float32 [768], replicated, may hold values from 0.25 to 1.75
- spatial_shift: float32 [768], replicated, may hold values from -1.75 to 1.75
- spatial_qkv: bfloat16 [768, 2304], replicated, may hold values from -0.21875 to 0.21875
- spatial_qv_bias: float32 [1536], replicated, may hold values from -1.75 to 1.75
- spatial_proj: bfloat16 [768, 768], replicated, may hold values from -2 to 2
- spatial_proj_bias: float32 [768], replicated, may hold values from -1.75 to 1.75
- mlp_gain: float32 [768], replicated, may hold values from 0.25 to 1.75
- mlp_shift: float32 [768], replicated, may hold values from -1.75 to 1.75
- fc1_weight: bfloat16 [768, 3072], P(None, 'mp'), may hold values from -0.21875 to 0.21875
- fc1_bias: bfloat16 [3072], P('mp'), may hold values from -1.75 to 1.75
- fc2_weight: bfloat16 [3072, 768], P('mp'), may hold values from -0.109375 to 0.109375
- fc2_bias: float32 [768], replicated, may hold values from -1.75 to 1.75
- cotangent: bfloat16 [8, 8, 784, 768], P('mp', 'dp'), may hold values from -6 to 6
Outputs:
- output: bfloat16 [8, 8, 784, 768], P('mp', 'dp')
- video_grad: float32 [8, 8, 784, 768], P('mp', 'dp')
- temporal_gain_grad: float32 [768], replicated
- temporal_shift_grad: float32 [768], replicated
- temporal_qkv_grad: float32 [768, 2304], replicated
- temporal_qv_bias_grad: float32 [1536], replicated
- temporal_proj_grad: float32 [768, 768], replicated
- temporal_proj_bias_grad: float32 [768], replicated
- spatial_gain_grad: float32 [768], replicated
- spatial_shift_grad: float32 [768], replicated
- spatial_qkv_grad: float32 [768, 2304], replicated
- spatial_qv_bias_grad: float32 [1536], replicated
- spatial_proj_grad: float32 [768, 768], replicated
- spatial_proj_bias_grad: float32 [768], replicated
- mlp_gain_grad: float32 [768], replicated
- mlp_shift_grad: float32 [768], replicated
- fc1_weight_grad: float32 [768, 3072], P('dp', 'mp')
- fc1_bias_grad: float32 [3072], replicated
- fc2_weight_grad: float32 [3072, 768], P('mp', 'dp')
- fc2_bias_grad: float32 [768], replicated
Inputs may be any that keep to these rules, and one draw needn't show every extreme that they name: `patch_width`: each set holds either one clip of 784 patches per frame or four clips of 196; sets of both kinds occur in every draw. Every clip has all 8 frames.
All inputs are finite; a program needn't handle non-finite values.
Results may differ from a plain program's by a relative error of at most 0.017.
Values may be sent and summed in bfloat16 or wider, within the bound.
A program may use at most 384 MiB of HBM per device.

v0:
```python
import jax
import jax.numpy as jnp
from jax import lax
from jax.sharding import PartitionSpec as P

HEADS = 12
HEAD_DIM = 64


EPSILON = 1e-06


def norm_forward(value, gain, shift):
    centered = value - jnp.mean(value, axis=-1, keepdims=True)
    scale = lax.rsqrt(jnp.mean(centered * centered, axis=-1, keepdims=True) + EPSILON)
    normed = centered * scale
    return (normed * gain + shift, normed, scale)


def norm_backward(grad, normed, scale, gain):
    width = grad.shape[-1]
    gain_grad = jnp.sum((grad * normed).reshape(-1, width), axis=0)
    shift_grad = jnp.sum(grad.reshape(-1, width), axis=0)
    inner = grad * gain
    result = scale * (
        inner
        - jnp.mean(inner, axis=-1, keepdims=True)
        - normed * jnp.mean(inner * normed, axis=-1, keepdims=True)
    )
    return (result, gain_grad, shift_grad)


def gelu_exact(value):
    return jax.nn.gelu(value, approximate=False)


def split_heads(joined, bias, width):
    queries = (joined[..., :width] + bias[:width]).astype(jnp.bfloat16)
    keys = joined[..., width : 2 * width].astype(jnp.bfloat16)
    values = (joined[..., 2 * width :] + bias[width:]).astype(jnp.bfloat16)
    shape = joined.shape[:-1] + (HEADS, HEAD_DIM)
    return (queries.reshape(shape), keys.reshape(shape), values.reshape(shape))


def temporal_forward(queries, keys, values):
    scores = jnp.einsum(
        "fnphe,gnphe->nphfg", queries, keys, preferred_element_type=jnp.float32
    ) * HEAD_DIM ** (-0.5)
    top = jnp.max(scores, axis=-1, keepdims=True)
    lifted = jnp.exp(scores - top)
    mixing = lifted / jnp.sum(lifted, axis=-1, keepdims=True)
    mixed = jnp.einsum(
        "nphfg,gnphe->fnphe",
        mixing.astype(jnp.bfloat16),
        values,
        preferred_element_type=jnp.float32,
    )
    return (mixed.astype(jnp.bfloat16), mixing)


def temporal_backward(queries, keys, values, mixing, grad_mixed):
    grad_values = jnp.einsum(
        "nphfg,fnphe->gnphe",
        mixing.astype(jnp.bfloat16),
        grad_mixed,
        preferred_element_type=jnp.float32,
    )
    grad_mixing = jnp.einsum(
        "fnphe,gnphe->nphfg", grad_mixed, values, preferred_element_type=jnp.float32
    )
    grad_scores = (
        mixing * (grad_mixing - jnp.sum(mixing * grad_mixing, axis=-1, keepdims=True))
    ).astype(jnp.bfloat16)
    grad_queries = jnp.einsum(
        "nphfg,gnphe->fnphe", grad_scores, keys, preferred_element_type=jnp.float32
    ) * HEAD_DIM ** (-0.5)
    grad_keys = jnp.einsum(
        "nphfg,fnphe->gnphe", grad_scores, queries, preferred_element_type=jnp.float32
    ) * HEAD_DIM ** (-0.5)
    return (
        grad_queries.astype(jnp.bfloat16),
        grad_keys.astype(jnp.bfloat16),
        grad_values.astype(jnp.bfloat16),
    )


def group_forward(queries, keys, values, groups):
    rows = queries.shape[0] // groups
    shape = (groups, rows) + queries.shape[1:]
    scores = jnp.einsum(
        "blhe,bmhe->bhlm",
        queries.reshape(shape),
        keys.reshape(shape),
        preferred_element_type=jnp.float32,
    ) * HEAD_DIM ** (-0.5)
    top = jnp.max(scores, axis=-1, keepdims=True)
    lifted = jnp.exp(scores - top)
    total = jnp.sum(lifted, axis=-1, keepdims=True)
    mixing = (lifted / total).astype(jnp.bfloat16)
    mixed = jnp.einsum(
        "bhlm,bmhe->blhe", mixing, values.reshape(shape), preferred_element_type=jnp.float32
    )
    logsum = jnp.swapaxes((top + jnp.log(total))[..., 0], 1, 2)
    return (
        mixed.astype(jnp.bfloat16).reshape(queries.shape),
        logsum.reshape(queries.shape[0], queries.shape[1]),
    )


def group_backward(queries, keys, values, grad_mixed, logsum, groups):
    rows = queries.shape[0] // groups
    shape = (groups, rows) + queries.shape[1:]
    query_group = queries.reshape(shape)
    key_group = keys.reshape(shape)
    grad_group = grad_mixed.reshape(shape)
    scores = jnp.einsum(
        "blhe,bmhe->bhlm", query_group, key_group, preferred_element_type=jnp.float32
    ) * HEAD_DIM ** (-0.5)
    row_logsum = jnp.swapaxes(logsum.reshape(groups, rows, -1), 1, 2)[..., None]
    mixing = jnp.exp(scores - row_logsum)
    grad_values = jnp.einsum(
        "bhlm,blhe->bmhe",
        mixing.astype(jnp.bfloat16),
        grad_group,
        preferred_element_type=jnp.float32,
    )
    grad_mixing = jnp.einsum(
        "blhe,bmhe->bhlm", grad_group, values.reshape(shape), preferred_element_type=jnp.float32
    )
    grad_scores = (
        mixing * (grad_mixing - jnp.sum(mixing * grad_mixing, axis=-1, keepdims=True))
    ).astype(jnp.bfloat16)
    grad_queries = jnp.einsum(
        "bhlm,bmhe->blhe", grad_scores, key_group, preferred_element_type=jnp.float32
    ) * HEAD_DIM ** (-0.5)
    grad_keys = jnp.einsum(
        "bhlm,blhe->bmhe", grad_scores, query_group, preferred_element_type=jnp.float32
    ) * HEAD_DIM ** (-0.5)
    return (
        grad_queries.astype(jnp.bfloat16).reshape(queries.shape),
        grad_keys.astype(jnp.bfloat16).reshape(queries.shape),
        grad_values.astype(jnp.bfloat16).reshape(queries.shape),
    )


def spatial_forward(queries, keys, values, widths):

    def item(inputs):
        query_item, key_item, value_item, width = inputs
        return lax.cond(
            width == query_item.shape[0],
            lambda: group_forward(query_item, key_item, value_item, 1),
            lambda: group_forward(query_item, key_item, value_item, 4),
        )

    return lax.map(item, (queries, keys, values, widths))


def spatial_backward(queries, keys, values, grad_mixed, logsum, widths):

    def item(inputs):
        query_item, key_item, value_item, grad_item, logsum_item, width = inputs
        return lax.cond(
            width == query_item.shape[0],
            lambda: group_backward(query_item, key_item, value_item, grad_item, logsum_item, 1),
            lambda: group_backward(query_item, key_item, value_item, grad_item, logsum_item, 4),
        )

    return lax.map(item, (queries, keys, values, grad_mixed, logsum, widths))


def shards(
    video,
    patch_width,
    temporal_gain,
    temporal_shift,
    temporal_qkv,
    temporal_qv_bias,
    temporal_proj,
    temporal_proj_bias,
    spatial_gain,
    spatial_shift,
    spatial_qkv,
    spatial_qv_bias,
    spatial_proj,
    spatial_proj_bias,
    mlp_gain,
    mlp_shift,
    fc1_weight,
    fc1_bias,
    fc2_weight,
    fc2_bias,
    cotangent,
):
    width = video.shape[-1]
    frames_local, sets_local, slots = (video.shape[0], video.shape[1], video.shape[2])
    inputs = video.astype(jnp.float32)
    normed_in, unit_in, scale_in = norm_forward(inputs, temporal_gain, temporal_shift)
    slot_rows = lax.all_to_all(
        normed_in.astype(jnp.bfloat16), "mp", split_axis=2, concat_axis=0, tiled=True
    )
    joined = jnp.dot(slot_rows, temporal_qkv, preferred_element_type=jnp.float32)
    time_query, time_key, time_value = split_heads(joined, temporal_qv_bias, width)
    time_mixed, time_mixing = temporal_forward(time_query, time_key, time_value)
    time_back = lax.all_to_all(
        time_mixed.reshape(slot_rows.shape), "mp", split_axis=0, concat_axis=2, tiled=True
    )
    first = (
        inputs
        + jnp.dot(time_back, temporal_proj, preferred_element_type=jnp.float32)
        + temporal_proj_bias
    )
    normed_mid, unit_mid, scale_mid = norm_forward(first, spatial_gain, spatial_shift)
    normed_mid = normed_mid.astype(jnp.bfloat16)
    joined = jnp.dot(normed_mid, spatial_qkv, preferred_element_type=jnp.float32)
    space_query, space_key, space_value = split_heads(joined, spatial_qv_bias, width)
    item_shape = (-1, slots, HEADS, HEAD_DIM)
    widths = jnp.broadcast_to(patch_width[None, :], (frames_local, sets_local)).reshape(-1)
    space_query = space_query.reshape(item_shape)
    space_key = space_key.reshape(item_shape)
    space_value = space_value.reshape(item_shape)
    space_mixed, space_logsum = spatial_forward(space_query, space_key, space_value, widths)
    space_mixed = space_mixed.reshape(video.shape)
    second = (
        first
        + jnp.dot(space_mixed, spatial_proj, preferred_element_type=jnp.float32)
        + spatial_proj_bias
    )
    normed_out, unit_out, scale_out = norm_forward(second, mlp_gain, mlp_shift)
    normed_out = normed_out.astype(jnp.bfloat16)
    grad_out = cotangent.astype(jnp.float32)
    fc2_bias_grad = jnp.sum(grad_out.reshape(-1, width), axis=0)
    group_rows = lax.all_gather(normed_out, "mp", axis=0, tiled=True)
    inner = jnp.dot(group_rows, fc1_weight, preferred_element_type=jnp.float32) + fc1_bias
    hidden_full, gelu_back = jax.vjp(gelu_exact, inner)
    hidden = hidden_full.astype(jnp.bfloat16)
    branch = lax.psum_scatter(
        jnp.dot(hidden, fc2_weight, preferred_element_type=jnp.float32).astype(jnp.bfloat16),
        "mp",
        scatter_dimension=0,
        tiled=True,
    ).astype(jnp.float32)
    output = second + branch + fc2_bias
    group_grad = lax.all_gather(cotangent, "mp", axis=0, tiled=True)
    units = hidden.shape[-1]
    fc2_part = jnp.einsum(
        "rf,rd->fd",
        hidden.reshape(-1, units),
        group_grad.reshape(-1, width),
        preferred_element_type=jnp.float32,
    )
    grad_hidden = jnp.einsum(
        "...d,fd->...f", group_grad, fc2_weight, preferred_element_type=jnp.float32
    )
    grad_inner = gelu_back(grad_hidden)[0].astype(jnp.bfloat16)
    fc1_part = jnp.einsum(
        "rd,rf->df",
        group_rows.reshape(-1, width),
        grad_inner.reshape(-1, units),
        preferred_element_type=jnp.float32,
    )
    local_bias = jnp.sum(grad_inner.reshape(-1, units).astype(jnp.float32), axis=0)
    owner = (jnp.arange(lax.axis_size("mp")) == lax.axis_index("mp")).astype(jnp.float32)
    fc1_bias_grad = (owner[:, None] * local_bias[None, :]).reshape(-1)
    grad_normed = lax.psum_scatter(
        jnp.einsum(
            "...f,df->...d", grad_inner, fc1_weight, preferred_element_type=jnp.float32
        ).astype(jnp.bfloat16),
        "mp",
        scatter_dimension=0,
        tiled=True,
    ).astype(jnp.float32)
    fc1_weight_grad, fc2_weight_grad = (
        lax.psum_scatter(
            fc1_part.astype(jnp.bfloat16), "dp", scatter_dimension=0, tiled=True
        ).astype(jnp.float32),
        lax.psum_scatter(
            fc2_part.astype(jnp.bfloat16), "dp", scatter_dimension=1, tiled=True
        ).astype(jnp.float32),
    )
    grad_norm_out, mlp_gain_grad, mlp_shift_grad = norm_backward(
        grad_normed, unit_out, scale_out, mlp_gain
    )
    grad_second = grad_out + grad_norm_out
    grad_space_out = grad_second.astype(jnp.bfloat16)
    spatial_proj_bias_grad = jnp.sum(grad_space_out.reshape(-1, width).astype(jnp.float32), axis=0)
    spatial_proj_grad = jnp.einsum(
        "rd,re->de",
        space_mixed.reshape(-1, width),
        grad_space_out.reshape(-1, width),
        preferred_element_type=jnp.float32,
    )
    grad_space = jnp.einsum(
        "...e,de->...d", grad_space_out, spatial_proj, preferred_element_type=jnp.float32
    ).astype(jnp.bfloat16)
    grad_space_query, grad_space_key, grad_space_value = spatial_backward(
        space_query, space_key, space_value, grad_space.reshape(item_shape), space_logsum, widths
    )
    grad_joined = jnp.concatenate(
        [
            grad_space_query.reshape(video.shape),
            grad_space_key.reshape(video.shape),
            grad_space_value.reshape(video.shape),
        ],
        axis=-1,
    )
    spatial_qkv_grad = jnp.einsum(
        "rd,rj->dj",
        normed_mid.reshape(-1, width),
        grad_joined.reshape(-1, 3 * width),
        preferred_element_type=jnp.float32,
    )
    spatial_qv_bias_grad = jnp.concatenate(
        [
            jnp.sum(grad_joined[..., :width].reshape(-1, width).astype(jnp.float32), axis=0),
            jnp.sum(grad_joined[..., 2 * width :].reshape(-1, width).astype(jnp.float32), axis=0),
        ]
    )
    grad_mid_normed = jnp.einsum(
        "...j,dj->...d", grad_joined, spatial_qkv, preferred_element_type=jnp.float32
    )
    grad_norm_mid, spatial_gain_grad, spatial_shift_grad = norm_backward(
        grad_mid_normed, unit_mid, scale_mid, spatial_gain
    )
    grad_first = grad_second + grad_norm_mid
    grad_time_out = grad_first.astype(jnp.bfloat16)
    temporal_proj_bias_grad = jnp.sum(grad_time_out.reshape(-1, width).astype(jnp.float32), axis=0)
    temporal_proj_grad = jnp.einsum(
        "rd,re->de",
        time_back.reshape(-1, width),
        grad_time_out.reshape(-1, width),
        preferred_element_type=jnp.float32,
    )
    grad_time = jnp.einsum(
        "...e,de->...d", grad_time_out, temporal_proj, preferred_element_type=jnp.float32
    ).astype(jnp.bfloat16)
    grad_slot = lax.all_to_all(grad_time, "mp", split_axis=2, concat_axis=0, tiled=True)
    head_shape = grad_slot.shape[:-1] + (HEADS, HEAD_DIM)
    grad_time_query, grad_time_key, grad_time_value = temporal_backward(
        time_query, time_key, time_value, time_mixing, grad_slot.reshape(head_shape)
    )
    grad_joined = jnp.concatenate(
        [
            grad_time_query.reshape(grad_slot.shape),
            grad_time_key.reshape(grad_slot.shape),
            grad_time_value.reshape(grad_slot.shape),
        ],
        axis=-1,
    )
    temporal_qkv_grad = jnp.einsum(
        "rd,rj->dj",
        slot_rows.reshape(-1, width),
        grad_joined.reshape(-1, 3 * width),
        preferred_element_type=jnp.float32,
    )
    temporal_qv_bias_grad = jnp.concatenate(
        [
            jnp.sum(grad_joined[..., :width].reshape(-1, width).astype(jnp.float32), axis=0),
            jnp.sum(grad_joined[..., 2 * width :].reshape(-1, width).astype(jnp.float32), axis=0),
        ]
    )
    grad_slot_normed = jnp.einsum(
        "...j,dj->...d", grad_joined, temporal_qkv, preferred_element_type=jnp.float32
    )
    grad_in_normed = lax.all_to_all(
        grad_slot_normed.astype(jnp.bfloat16), "mp", split_axis=0, concat_axis=2, tiled=True
    ).astype(grad_slot_normed.dtype)
    grad_norm_in, temporal_gain_grad, temporal_shift_grad = norm_backward(
        grad_in_normed, unit_in, scale_in, temporal_gain
    )
    video_grad = grad_first + grad_norm_in
    summed = lax.psum(
        (
            temporal_gain_grad,
            temporal_shift_grad,
            temporal_qkv_grad,
            temporal_qv_bias_grad,
            temporal_proj_grad,
            temporal_proj_bias_grad,
            spatial_gain_grad,
            spatial_shift_grad,
            spatial_qkv_grad,
            spatial_qv_bias_grad,
            spatial_proj_grad,
            spatial_proj_bias_grad,
            mlp_gain_grad,
            mlp_shift_grad,
            fc1_bias_grad,
            fc2_bias_grad,
        ),
        ("dp", "mp"),
    )
    return (
        output.astype(jnp.bfloat16),
        video_grad,
        summed[0],
        summed[1],
        summed[2],
        summed[3],
        summed[4],
        summed[5],
        summed[6],
        summed[7],
        summed[8],
        summed[9],
        summed[10],
        summed[11],
        summed[12],
        summed[13],
        fc1_weight_grad,
        summed[14],
        fc2_weight_grad,
        summed[15],
    )


def solution(mesh):
    return jax.shard_map(
        shards,
        mesh=mesh,
        in_specs=(
            P("mp", "dp", None, None),
            P("dp"),
            P(),
            P(),
            P(),
            P(),
            P(),
            P(),
            P(),
            P(),
            P(),
            P(),
            P(),
            P(),
            P(),
            P(),
            P(None, "mp"),
            P("mp"),
            P("mp", None),
            P(),
            P("mp", "dp", None, None),
        ),
        out_specs=(
            P("mp", "dp", None, None),
            P("mp", "dp", None, None),
            P(),
            P(),
            P(),
            P(),
            P(),
            P(),
            P(),
            P(),
            P(),
            P(),
            P(),
            P(),
            P(),
            P(),
            P("dp", "mp"),
            P(),
            P("mp", "dp"),
            P(),
        ),
        check_vma=False,
    )
```

profile of v0, /device:TPU:0, one launch (start us, length us, event | category | flops | bytes accessed | tf_op | source)
XLA Modules:
  0.0 1836.4 jit_solution(13008250649940435090)
XLA Ops:
  24.1 54.9 %all-to-all-done = bf16[2,1,784,768]{3,0,1,2:T(2,128)(2,1)} async-done(((bf16[2,1,784,768]{3,0,1,2:T(2,128)(2,1)}), bf16[2,1,784,768]{3,0,1,2:T(2,128)(2,1)}, u32[]{:S(2)}, u32[]{:S(2)}) %all-to-all-start) | async-done | bytes 2408480 | tf_op jit(solution)/shard_map/all_to_all | solution.py:199
  130.0 15.5 fusion.159
  172.9 54.8 %all-to-all-done.1 = bf16[8,1,196,768]{3,2,1,0:T(8,128)(2,1)} async-done(((bf16[8,1,196,768]{3,2,1,0:T(8,128)(2,1)}), bf16[8,1,196,768]{3,2,1,0:T(8,128)(2,1)}, u32[]{:S(2)}, u32[]{:S(2)}) %all-to-all-start.1) | async-done | bytes 2408480 | tf_op jit(solution)/shard_map/all_to_all | solution.py:205
  268.0 107.7 %while.26 = (s32[]{:T(128)}, bf16[2,784,12,64]{1,3,2,0:T(8,128)(2,1)}, f32[2,784,12]{1,2,0:T(8,128)}, s32[2]{0:T(128)S(1)}, bf16[2,784,12,64]{1,3,2,0:T(8,128)(2...) while((s32[]{:T(128)}, ...), condition=%wide.region_13.14_spmd, body=%wide.region_6.13_spmd.sunk | while | flops 1955198720 | bytes 108538064 | solution.py:156
  275.5 42.3 %conditional.4 = (bf16[1,784,12,64]{1,3,2,0:T(8,128)(2,1)}, f32[1,784,12]{1,2,0:T(8,128)}) conditional(s32[]{:T(128)} %bitcast.360, (bf16[784,12,64]{0,2,1:T(8,128)(2,1)}, bf16[784,12,64]{0,2,1:T(8,128)(2,1)}, bf16[784,12,64]{0,2,1:T(8,128)(2,1)}) %tuple.119, (bf16[784,12,64]{0,2,1:T(8,128)(2,1)}, bf16[784,12,64]{0,2,1:T(8,128)(2,1)}, ...), branch_computations={%region_7.9_spmd, %region_10.12_spmd} | conditional | flops 1955198720 | bytes 98445360 | solution.py:150
  329.1 42.3 %conditional.4 = (bf16[1,784,12,64]{1,3,2,0:T(8,128)(2,1)}, f32[1,784,12]{1,2,0:T(8,128)}) conditional(s32[]{:T(128)} %bitcast.360, (bf16[784,12,64]{0,2,1:T(8,128)(2,1)}, bf16[784,12,64]{0,2,1:T(8,128)(2,1)}, bf16[784,12,64]{0,2,1:T(8,128)(2,1)}) %tuple.119, (bf16[784,12,64]{0,2,1:T(8,128)(2,1)}, bf16[784,12,64]{0,2,1:T(8,128)(2,1)}, ...), branch_computations={%region_7.9_spmd, %region_10.12_spmd} | conditional | flops 1955198720 | bytes 98445360 | solution.py:150
  387.9 177.1 %all-gather.3.cloned.1.call-done = bf16[8,1,784,768]{3,2,1,0:T(8,128)(2,1)} async-done(((bf16[2,1,784,768]{3,2,1,0:T(8,128)(2,1)}), bf16[8,1,784,768]{3,2,1,0:T(8,128)(2,1)}) %all-gather.3.cloned.1.call-update) | async-done | bytes 9633808 | tf_op jit(solution)/shard_map/all_gather | solution.py:233
  565.0 21.0 %fusion.110 = (u8[784,768]{1,0:T(8,128)(4,1)S(1)}, u8[784,768]{1,0:T(8,128)(4,1)S(1)}, f32[8,784,768]{2,1,0:T(8,128)}) fusion(f32[768]{0:T(1024)} %convert_element_type.330, bf16[768,768]{1,0:T(8,128)(2,1)} %param.45, bf16[8,1,784,768]{3,2,1,0:T(8,128)(2,1)} %all-gather.3.cloned.1.call-done), kind=kOutput, calls=%fused_computation.189 | convolution fusion | flops 7464984576 | bytes 31288320 | tf_op jit(solution)/shard_map/dot_general | solution.py:234
  586.0 47.0 %multiply_convert_fusion.6 = (bf16[8,784,768]{2,1,0:T(8,128)(2,1)}, f32[8,784,768]{2,1,0:T(8,128)}) fusion(f32[8,784,768]{2,1,0:T(8,128)} %get-tuple-element.431, f32[768]{0:T(1024)S(1)} %copy-done.54, u8[784,768]{1,0:T(8,128)(4,1)S(1)} %get-tuple-element.331, u8[784,768]{1,0:T(8,128)(4,1)S(1)} %get-tuple-element.330), kind=kLoop, calls=%fused_computation.74 | loop fusion | flops 341999616 | bytes 49376256 | tf_op jit(solution)/shard_map/convert_element_type | solution.py:236
  632.9 101.8 %all-gather.5.cloned.1.call-done = bf16[8,1,784,768]{3,2,1,0:T(8,128)(2,1)} async-done(((bf16[2,1,784,768]{3,2,1,0:T(8,128)(2,1)}), bf16[8,1,784,768]{3,2,1,0:T(8,128)(2,1)}) %all-gather.5.cloned.1.call-update) | async-done | bytes 9633808 | tf_op jit(solution)/shard_map/all_gather | solution.py:244
  734.8 26.2 %convert_reduce_fusion = (f32[768]{0:T(1024)}, bf16[8,784,768]{2,1,0:T(8,128)(2,1)}) fusion(f32[8,784,768]{2,1,0:T(8,128)} %get-tuple-element.400, bf16[768,768]{1,0:T(8,128)(2,1)} %param.47, bf16[8,1,784,768]{3,2,1,0:T(8,128)(2,1)} %all-gather.5.cloned.1.call-done, f32[8,784,768]{2,1,0:T(8,128)} %get-tuple-element.431, f32[768]{0:T(1024)} %convert_element_type.330), kind=kOutput, calls=%fused_computation.72 | convolution fusion | flops 7480638464 | bytes 58988544 | tf_op jit(solution)/shard_map/...d,fd->...f/dot_general | solution.py:252
  761.0 13.6 convert_bitcast_fusion
  774.7 12.8 convert_bitcast_fusion.1
  808.9 14.2 bitcast_convert_fusion
  823.1 114.4 %reduce-scatter.7.cloned.1.call-done = bf16[2,1,784,768]{3,2,0,1:T(8,128)(2,1)} async-done(((bf16[8,1,784,768]{3,2,0,1:T(8,128)(2,1)}), bf16[2,1,784,768]{3,2,0,1:T(8,128)(2,1)}) %reduce-scatter.7.cloned.1.call-update) | async-done | bytes 2408464 | tf_op jit(solution)/shard_map/reduce_scatter | solution.py:265
  962.2 256.0 %while.27 = (s32[]{:T(128)}, bf16[2,784,12,64]{1,3,2,0:T(8,128)(2,1)}, bf16[2,784,12,64]{1,3,2,0:T(8,128)(2,1)}, bf16[2,784,12,64]{1,3,2,0:T(8,128)(2,1)}, s32[2...) while((s32[]{:T(128)}, ...), condition=%wide.region_25.26_spmd, body=%wide.region_20.0_spmd.sunk | while | flops 4812069888 | bytes 299642528 | solution.py:169
  971.1 108.6 %conditional.5 = (bf16[1,784,12,64]{1,3,2,0:T(8,128)(2,1)}, bf16[1,784,12,64]{1,3,2,0:T(8,128)(2,1)}, bf16[1,784,12,64]{1,3,2,0:T(8,128)(2,1)}) conditional(s32[]{:T(128)} %bitcast.364, (bf16[784,12,64]{0,2,1:T(8,128)(2,1)}, bf16[784,12,64]{0,2,1:T(8,128)(2,1)}, f32[784,12]{0,1:T(8,128)}, bf16[784,12,64]{0,2,1:T(8,128)(2,1)}, ...), branch_computations={%region_21.22_spmd, %region_23.24_spmd} | conditional | flops 4812069888 | bytes 238323520 | solution.py:163
  1025.2 12.4 multiply_reduce_fusion.2
  1037.6 11.7 multiply_convert_fusion
  1095.8 108.0 %conditional.5 = (bf16[1,784,12,64]{1,3,2,0:T(8,128)(2,1)}, bf16[1,784,12,64]{1,3,2,0:T(8,128)(2,1)}, bf16[1,784,12,64]{1,3,2,0:T(8,128)(2,1)}) conditional(s32[]{:T(128)} %bitcast.364, (bf16[784,12,64]{0,2,1:T(8,128)(2,1)}, bf16[784,12,64]{0,2,1:T(8,128)(2,1)}, f32[784,12]{0,1:T(8,128)}, bf16[784,12,64]{0,2,1:T(8,128)(2,1)}, ...), branch_computations={%region_21.22_spmd, %region_23.24_spmd} | conditional | flops 4812069888 | bytes 238323520 | solution.py:163
  1149.9 12.0 multiply_reduce_fusion.2
  1161.9 11.6 multiply_convert_fusion
  1231.7 11.4 fusion.103
  1247.0 12.3 convert_reduce_fusion.9
  1270.8 14.3 bitcast_convert_fusion.1
  1295.4 10.4 convolution_bitcast_fusion.2
  1305.8 19.4 %all-to-all-done.2 = bf16[2,1,784,768]{3,0,1,2:T(2,128)(2,1)} async-done(((bf16[2,1,784,768]{3,0,1,2:T(2,128)(2,1)}), bf16[2,1,784,768]{3,0,1,2:T(2,128)(2,1)}, u32[]{:S(2)}, u32[]{:S(2)}) %all-to-all-start.2) | async-done | bytes 2408480 | tf_op jit(solution)/shard_map/all_to_all | solution.py:337
  1350.1 12.9 multiply_reduce_fusion.4
  1434.5 13.5 fusion.61
  1515.9 67.0 %all-to-all-done.3 = bf16[8,1,196,768]{3,2,1,0:T(8,128)(2,1)} async-done(((bf16[8,1,196,768]{3,2,1,0:T(8,128)(2,1)}), bf16[8,1,196,768]{3,2,1,0:T(8,128)(2,1)}, u32[]{:S(2)}, u32[]{:S(2)}) %all-to-all-start.3) | async-done | bytes 2408480 | tf_op jit(solution)/shard_map/all_to_all | solution.py:365
  1605.8 53.2 %all-reduce = (f32[768]{0:T(1024)}, f32[768]{0:T(1024)}, f32[1536]{0:T(1024)}, f32[768]{0:T(1024)}, f32[768]{0:T(1024)}, /*index=5*/f32[768]{0:T(1024)}, f32[153...) all-reduce(f32[768]{0:T(1024)} %get-tuple-element.336, ...), channel_id=1, replica_groups=mesh['dp'=8,'mp'=4] {'dp','mp'}, use_global_device_ids=true, to_apply=%region_32.33 | all-reduce | flops 13056 | bytes 104448 | tf_op jit(solution)/shard_map/psum | solution.py:372
  1666.5 149.4 %all-reduce.4.cloned.1.call-done = (f32[768,2304]{1,0:T(8,128)}, f32[768,768]{1,0:T(8,128)}, f32[768,2304]{1,0:T(8,128)}, f32[768,768]{1,0:T(8,128)}) async-done(((f32[768,2304]{1,0:T(8,128)}, f32[768,768]{1,0:T(8,128)}, f32[768,2304]{1,0:T(8,128)}, f32[768,768]{1,0:T(8,128)}), (f32[768,2304]{1,0:T(8,128)}, f32[768,768]{1,0:T(8,128)}, f32[768,2304]{1,0:T(8,128)}, ...) | async-done | bytes 18874384 | tf_op jit(solution)/shard_map/psum | solution.py:372
  (386 shorter events, 725.2 us)
Async XLA Ops:
  7.2 234.2 %copy-start = (bf16[768,2304]{1,0:T(8,128)(2,1)S(1)}, bf16[768,2304]{1,0:T(8,128)(2,1)}, u32[]{:S(2)}) copy-start(bf16[768,2304]{1,0:T(8,128)(2,1)} %param.39) | copy-start | bytes 10616836
  13.9 10.2 copy-start.58
  17.2 61.8 %all-to-all-start = ((bf16[2,1,784,768]{3,0,1,2:T(2,128)(2,1)}), bf16[2,1,784,768]{3,0,1,2:T(2,128)(2,1)}, u32[]{:S(2)}, u32[]{:S(2)}) async-start(bf16[2,1,784,768]{3,0,1,2:T(2,128)(2,1)} %copy.366), calls=%async_computation | async-start | bytes 4816896 | tf_op jit(solution)/shard_map/all_to_all | solution.py:199
  163.1 9.8 copy-start.59
  167.6 60.1 %all-to-all-start.1 = ((bf16[8,1,196,768]{3,2,1,0:T(8,128)(2,1)}), bf16[8,1,196,768]{3,2,1,0:T(8,128)(2,1)}, u32[]{:S(2)}, u32[]{:S(2)}) async-start(bf16[8,1,196,768]{3,2,1,0:T(8,128)(2,1)} %copy.378), calls=%async_computation.1 | async-start | bytes 4915200 | tf_op jit(solution)/shard_map/all_to_all | solution.py:205
  172.2 392.8 %all-gather.3.cloned.1.call-start = ((), (), s32[]{:S(2)}) async-start(), calls=%async_computation.8 | async-start | bytes 12042240 | tf_op jit(solution)/shard_map/all_gather | solution.py:233
  227.7 7.7 copy-start.66
  268.0 107.8 %copy-start.67 = (f32[768]{0:T(1024)S(1)}, f32[768]{0:T(1024)}, u32[]{:S(2)}) copy-start(f32[768]{0:T(1024)} %param.42) | copy-start | bytes 9220
  381.7 560.8 %copy-start.33 = (f32[2,784]{1,0:T(2,128)}, f32[2,784]{1,0:T(2,128)S(1)}, u32[]{:S(2)}) copy-start(f32[2,784]{1,0:T(2,128)S(1)} %broadcast_multiply_fusion.6) | copy-start | bytes 18820
  383.8 558.7 %copy-start.37 = (f32[2,784]{1,0:T(2,128)}, f32[2,784]{1,0:T(2,128)S(1)}, u32[]{:S(2)}) copy-start(f32[2,784]{1,0:T(2,128)S(1)} %add_rsqrt_fusion) | copy-start | bytes 18820
  385.8 349.0 %all-gather.5.cloned.1.call-start = ((), (), s32[]{:S(2)}) async-start(), calls=%async_computation.10 | async-start | bytes 12042240 | tf_op jit(solution)/shard_map/all_gather | solution.py:244
  386.5 550.9 %reduce-scatter.7.cloned.1.call-start = ((), (), s32[]{:S(2)}) async-start(), calls=%async_computation.11 | async-start | bytes 12042240 | tf_op jit(solution)/shard_map/reduce_scatter | solution.py:265
  565.0 21.0 %copy-start.54 = (f32[768]{0:T(1024)S(1)}, f32[768]{0:T(1024)}, u32[]{:S(2)}) copy-start(f32[768]{0:T(1024)} %convert_element_type.330) | copy-start | bytes 9220
  734.8 26.3 %copy-start.63 = (bf16[768,768]{1,0:T(8,128)(2,1)S(1)}, bf16[768,768]{1,0:T(8,128)(2,1)}, u32[]{:S(2)}) copy-start(bf16[768,768]{1,0:T(8,128)(2,1)} %param.45) | copy-start | bytes 3538948
  774.7 472.3 %reduce-scatter.5.cloned.1.call-start = ((), (), s32[]{:S(2)}) async-start(), calls=%async_computation.9 | async-start | bytes 12042240 | tf_op jit(solution)/shard_map/reduce_scatter | solution.py:237
  787.5 713.3 %reduce-scatter.11.cloned.1.call-start = ((), (), s32[]{:S(2)}) async-start(), calls=%async_computation.13 | async-start | bytes 1327104 | tf_op jit(solution)/shard_map/reduce_scatter | solution.py:277
  1222.7 9.0 copy-start.46
  1222.7 9.0 copy-start.52
  1231.7 13.6 copy-start.56
  1247.0 13.8 copy-start.65
  1266.2 59.1 %all-to-all-start.2 = ((bf16[2,1,784,768]{3,0,1,2:T(2,128)(2,1)}), bf16[2,1,784,768]{3,0,1,2:T(2,128)(2,1)}, u32[]{:S(2)}, u32[]{:S(2)}) async-start(bf16[2,1,784,768]{3,0,1,2:T(2,128)(2,1)} %copy.390), calls=%async_computation.4 | async-start | bytes 4816896 | tf_op jit(solution)/shard_map/all_to_all | solution.py:337
  1270.7 231.7 %reduce-scatter.9.cloned.1.call-start = ((), (), s32[]{:S(2)}) async-start(), calls=%async_computation.12 | async-start | bytes 1327104 | tf_op jit(solution)/shard_map/reduce_scatter | solution.py:274
  1285.1 530.8 %all-reduce.4.cloned.1.call-start = ((), (), s32[]{:S(2)}) async-start(), calls=%async_computation.14 | async-start | bytes 37748736 | tf_op jit(solution)/shard_map/psum | solution.py:372
  1285.2 10.1 slice-start
  1372.4 9.0 copy-start.14
  1494.7 88.2 %copy-start.44 = (f32[768]{0:T(1024)S(1)}, f32[768]{0:T(1024)}, u32[]{:S(2)}) copy-start(f32[768]{0:T(1024)} %param.31) | copy-start | bytes 9220
  1494.7 88.2 %all-to-all-start.3 = ((bf16[8,1,196,768]{3,2,1,0:T(8,128)(2,1)}), bf16[8,1,196,768]{3,2,1,0:T(8,128)(2,1)}, u32[]{:S(2)}, u32[]{:S(2)}) async-start(bf16[8,1,196,768]{3,2,1,0:T(8,128)(2,1)} %convert_bitcast_fusion.4), calls=%async_computation.5 | async-start | bytes 4915200 | tf_op jit(solution)/shard_map/all_to_all | solution.py:365
  1500.8 13.2 copy-start.50
  1593.1 8.0 copy-start.36
  1593.1 8.0 copy-start.40
  1815.9 7.2 copy-start.32
  1815.9 8.6 copy-start.23
  (63 other events, 266.9 us)
Sparse Core Ops, SparseCore 0:
  385.9 179.0 all-gather.2
  566.5 168.1 all-gather.4
  774.8 162.5 reduce-scatter.6
  939.6 165.2 reduce-scatter.4
  1108.0 37.6 reduce-scatter.10
  1285.2 47.2 reduce-scatter.8
  1448.2 367.7 all-reduce.3
where the time goes:
time: 1850 us; the launch traced here: 1840 us
  waiting for transfers between devices  740 us (40%)
  local copies, waits for them, and re-layouts  497 us (27%)
  matrix products  322 us (17%)
  other arithmetic  157 us (8%)
  blocking collectives  53.2 us (3%)
  loops' own time  30.6 us (2%)
  starting transfers between devices  20.9 us (1%)
    all_gather x1, waiting for transfers between devices, shards(): group_rows = lax.all_gather(normed_out, 'mp', axis=0, tiled=True)  177 us
    psum x1, waiting for transfers between devices, shards(): lax.psum((temporal_gain_grad, temporal_shift_grad, temporal_qkv_grad, tem...  149 us
    another operation x23, local copies, waits for them, and re-layouts  121 us
    reduce_scatter x1, waiting for transfers between devices, shards(): lax.psum_scatter(jnp.einsum('...f,df->...d', grad_inner, fc1_weight, pref...  114 us
    all_gather x1, waiting for transfers between devices, shards(): group_grad = lax.all_gather(cotangent, 'mp', axis=0, tiled=True)  102 us
    all_to_all x1, waiting for transfers between devices, shards(): lax.all_to_all(grad_slot_normed.astype(jnp.bfloat16), 'mp', split_axis=0,...  67 us
    all_to_all x1, waiting for transfers between devices, shards(): lax.all_to_all(normed_in.astype(jnp.bfloat16), 'mp', split_axis=2, concat...  54.9 us
    all_to_all x1, waiting for transfers between devices, shards(): lax.all_to_all(time_mixed.reshape(slot_rows.shape), 'mp', split_axis=0, c...  54.8 us
  transfers between devices with their start and end apart: 11, of which 8 were waited for; matrix products, arithmetic and copies ran while one was open for 36% of the time, Pallas kernels for 0%

commit v1 on v0

v1 whole, which is shorter than its diff:
```python
import functools
import jax
import jax.numpy as jnp
from jax import lax
from jax.experimental import pallas as pl
from jax.experimental.pallas import tpu as pltpu
from jax.sharding import PartitionSpec as P

HEADS = 12
HEAD_DIM = 64
GROUP = 4
WIDE = GROUP * HEAD_DIM
EPSILON = 1e-06
F32 = jnp.float32
BF16 = jnp.bfloat16
MIB = 1 << 20


def params(mib=56):
    return pltpu.CompilerParams(vmem_limit_bytes=mib * MIB)


def dot(a, b):
    return jnp.dot(a, b, preferred_element_type=F32)


def dot_nt(a, b):
    return lax.dot_general(a, b, (((1,), (1,)), ((), ())), preferred_element_type=F32)


def dot_tn(a, b):
    return lax.dot_general(a, b, (((0,), (0,)), ((), ())), preferred_element_type=F32)


def head_lanes(rows, head, dtype):
    lane = lax.broadcasted_iota(jnp.int32, (rows, WIDE), 1)
    return (lane // HEAD_DIM == head).astype(dtype)


def windows(slots, clips, rows):
    size = slots // clips
    found = []
    for start in range(0, slots, rows):
        stop = min(start + rows, slots)
        low = start // size * size // 16 * 16
        high = min(-(-(-(-stop // size) * size) // 16) * 16, slots)
        found.append((start, stop, low, high))
    return found


def spatial_fwd_body(width_ref, q_ref, k_ref, v_ref, o_ref, l_ref, *, slots, rows, narrow):
    def attend(chunks, size):
        stats = []
        for start, stop, low, high in chunks:
            count = stop - start
            q = q_ref[start:stop, :]
            k = k_ref[low:high, :]
            v = v_ref[low:high, :]
            if size < slots:
                query_clip = (lax.broadcasted_iota(jnp.int32, (count, high - low), 0) + start) // size
                key_clip = (lax.broadcasted_iota(jnp.int32, (count, high - low), 1) + low) // size
                same = query_clip == key_clip
            total = jnp.zeros((count, WIDE), F32)
            lse = jnp.zeros((count, 128), F32)
            lane = lax.broadcasted_iota(jnp.int32, (count, 128), 1)
            for head in range(GROUP):
                s = dot_nt(q * head_lanes(count, head, BF16), k)
                if size < slots:
                    s = jnp.where(same, s, -1e30)
                top = jnp.max(s, axis=1, keepdims=True)
                e = jnp.exp(s - top)
                norm = jnp.sum(e, axis=1, keepdims=True)
                o = dot(e.astype(BF16), v)
                total = total + o * (head_lanes(count, head, F32) / norm)
                lse = jnp.where(lane == head, top + jnp.log(norm), lse)
            o_ref[start:stop, :] = total.astype(BF16)
            stats.append(lse)
        l_ref[...] = jnp.concatenate(stats, axis=0).T[:8, :]

    wide = width_ref[0] == slots

    @pl.when(wide)
    def _():
        attend(windows(slots, 1, rows or slots), slots)

    @pl.when(jnp.logical_not(wide))
    def _():
        attend(windows(slots, 4, narrow), slots // 4)


def spatial_fwd(width, qkv, frames, slots, rows=None, narrow=256):
    groups = HEADS // GROUP
    qkv = qkv.reshape(frames, slots, -1)
    spec = lambda part: pl.BlockSpec((None, slots, WIDE), lambda f, g, w: (f, 0, part * groups + g))
    out = pl.pallas_call(
        functools.partial(spatial_fwd_body, slots=slots, rows=rows, narrow=narrow),
        grid_spec=pltpu.PrefetchScalarGridSpec(
            num_scalar_prefetch=1,
            grid=(frames, groups),
            in_specs=[spec(0), spec(1), spec(2)],
            out_specs=[
                pl.BlockSpec((None, slots, WIDE), lambda f, g, w: (f, 0, g)),
                pl.BlockSpec((None, None, 8, slots), lambda f, g, w: (f, g, 0, 0)),
            ],
        ),
        out_shape=[
            jax.ShapeDtypeStruct((frames, slots, HEADS * HEAD_DIM), BF16),
            jax.ShapeDtypeStruct((frames, groups, 8, slots), F32),
        ],
        compiler_params=params(),
        name="spatial_fwd",
    )(width, qkv, qkv, qkv)
    return out


def spatial_bwd_body(width_ref, q_ref, k_ref, v_ref, o_ref, l_ref, g_ref, dq_ref, dk_ref, dv_ref, dqt, *, slots, rows, narrow):
    prod = g_ref[...].astype(F32) * o_ref[...].astype(F32)
    high_part = prod.astype(BF16)
    low_part = (prod - high_part.astype(F32)).astype(BF16)
    lane = lax.broadcasted_iota(jnp.int32, (8, WIDE), 1)
    row = lax.broadcasted_iota(jnp.int32, (8, WIDE), 0)
    picks = (lane // HEAD_DIM == row).astype(BF16)
    delta = dot_nt(picks, high_part) + dot_nt(picks, low_part)

    def attend(chunks, size):
        dqt[...] = jnp.zeros_like(dqt)
        kt = k_ref[...].T
        for start, stop, low, high in chunks:
            count = stop - start
            k = k_ref[start:stop, :]
            v = v_ref[start:stop, :]
            q = q_ref[low:high, :]
            g = g_ref[low:high, :]
            if size < slots:
                key_clip = (lax.broadcasted_iota(jnp.int32, (count, high - low), 0) + start) // size
                query_clip = (lax.broadcasted_iota(jnp.int32, (count, high - low), 1) + low) // size
                same = query_clip == key_clip
            dk = jnp.zeros((count, WIDE), F32)
            dv = jnp.zeros((count, WIDE), F32)
            for head in range(GROUP):
                mask = head_lanes(count, head, BF16)
                s = dot_nt(k * mask, q)
                p = jnp.exp(s - l_ref[head : head + 1, low:high])
                if size < slots:
                    p = jnp.where(same, p, 0.0)
                dp = dot_nt(v * mask, g)
                ds = (p * (dp - delta[head : head + 1, low:high])).astype(BF16)
                keep = head_lanes(count, head, F32)
                dv = dv + dot(p.astype(BF16), g) * keep
                dk = dk + dot(ds, q) * keep
                span = slice(head * HEAD_DIM, (head + 1) * HEAD_DIM)
                dqt[span, low:high] += dot(kt[span, start:stop], ds)
            dk_ref[start:stop, :] = dk.astype(BF16)
            dv_ref[start:stop, :] = dv.astype(BF16)
        dq_ref[...] = (dqt[...] * HEAD_DIM**-0.5).T.astype(BF16)

    wide = width_ref[0] == slots

    @pl.when(wide)
    def _():
        attend(windows(slots, 1, rows or slots), slots)

    @pl.when(jnp.logical_not(wide))
    def _():
        attend(windows(slots, 4, narrow), slots // 4)


def spatial_bwd(width, qkv, mixed, lse, grad, frames, slots, rows=None, narrow=208):
    groups = HEADS // GROUP
    width_all = HEADS * HEAD_DIM
    qkv = qkv.reshape(frames, slots, -1)
    spec = lambda part: pl.BlockSpec((None, slots, WIDE), lambda f, g, w: (f, 0, part * groups + g))
    one = pl.BlockSpec((None, slots, WIDE), lambda f, g, w: (f, 0, g))
    out = pl.pallas_call(
        functools.partial(spatial_bwd_body, slots=slots, rows=rows, narrow=narrow),
        grid_spec=pltpu.PrefetchScalarGridSpec(
            num_scalar_prefetch=1,
            grid=(frames, groups),
            in_specs=[
                spec(0), spec(1), spec(2), one,
                pl.BlockSpec((None, None, 8, slots), lambda f, g, w: (f, g, 0, 0)), one,
            ],
            out_specs=[one, one, one],
            scratch_shapes=[pltpu.VMEM((WIDE, slots), F32)],
        ),
        out_shape=[jax.ShapeDtypeStruct((frames, slots, width_all), BF16)] * 3,
        compiler_params=params(),
        name="spatial_bwd",
    )(width, qkv, qkv, qkv, mixed, lse, grad)
    return out


def fixed(shape):
    return pl.BlockSpec(shape, lambda *_: (0,) * len(shape))


def norm_parts(value):
    centered = value - jnp.mean(value, axis=-1, keepdims=True)
    scale = lax.rsqrt(jnp.mean(centered * centered, axis=-1, keepdims=True) + EPSILON)
    return centered * scale, scale


def norm_grad(grad, unit, scale, gain):
    inner = grad * gain
    return scale * (
        inner
        - jnp.mean(inner, axis=-1, keepdims=True)
        - unit * jnp.mean(inner * unit, axis=-1, keepdims=True)
    )


def column_sum(value):
    return jnp.sum(value.astype(F32), axis=0, keepdims=True)


def norm_in_body(video_ref, gain_ref, shift_ref, out_ref):
    unit, _ = norm_parts(video_ref[...].astype(F32))
    slots = video_ref.shape[0]
    out_ref[:slots, :] = (unit * gain_ref[...] + shift_ref[...]).astype(BF16)
    if out_ref.shape[0] > slots:
        out_ref[slots:, :] = jnp.zeros((out_ref.shape[0] - slots, out_ref.shape[1]), BF16)


def norm_in(video, gain, shift, padded):
    frames, slots, width = video.shape
    return pl.pallas_call(
        norm_in_body,
        grid=(frames,),
        in_specs=[pl.BlockSpec((None, slots, width), lambda f: (f, 0, 0)), fixed((1, width)), fixed((1, width))],
        out_specs=pl.BlockSpec((None, padded, width), lambda f: (f, 0, 0)),
        out_shape=jax.ShapeDtypeStruct((frames, padded, width), BF16),
        compiler_params=params(),
        name="norm_in",
    )(video, gain, shift)


STEP = 16


def stacked(block, rows):
    return jnp.concatenate([block * head_lanes(rows, head, BF16) for head in range(GROUP)], axis=0)


def temporal_fwd_body(x_ref, wq_ref, wk_ref, wv_ref, bq_ref, bv_ref, q_ref, k_ref, v_ref, o_ref):
    frames, slots, width = x_ref.shape
    x = x_ref[...].reshape(frames * slots, width)
    shape = (frames, slots, WIDE)
    q_ref[...] = ((dot(x, wq_ref[...]) + bq_ref[...]) * HEAD_DIM**-0.5).astype(BF16).reshape(shape)
    k_ref[...] = dot(x, wk_ref[...]).astype(BF16).reshape(shape)
    v_ref[...] = (dot(x, wv_ref[...]) + bv_ref[...]).astype(BF16).reshape(shape)
    rows = frames * STEP
    row = lax.broadcasted_iota(jnp.int32, (rows, rows), 0)
    col = lax.broadcasted_iota(jnp.int32, (rows, rows), 1)
    same = row % STEP == col % STEP
    for step in range(slots // STEP):
        part = slice(step * STEP, (step + 1) * STEP)
        q = q_ref[:, part, :].reshape(rows, WIDE)
        keys = stacked(k_ref[:, part, :].reshape(rows, WIDE), rows)
        values = stacked(v_ref[:, part, :].reshape(rows, WIDE), rows)
        scores = dot_nt(q, keys)
        mixing = []
        for head in range(GROUP):
            s = jnp.where(same, scores[:, head * rows : (head + 1) * rows], -1e30)
            e = jnp.exp(s - jnp.max(s, axis=1, keepdims=True))
            mixing.append((e / jnp.sum(e, axis=1, keepdims=True)).astype(BF16))
        o = dot(jnp.concatenate(mixing, axis=1), values)
        o_ref[:, part, :] = o.astype(BF16).reshape(frames, STEP, WIDE)


def temporal_fwd(x, weight, bias):
    frames, slots, width = x.shape
    groups = width // WIDE
    w = lambda part: pl.BlockSpec((width, WIDE), lambda g: (0, part * groups + g))
    b = lambda part: pl.BlockSpec((1, WIDE), lambda g: (0, part * groups + g))
    one = pl.BlockSpec((frames, slots, WIDE), lambda g: (0, 0, g))
    return pl.pallas_call(
        temporal_fwd_body,
        grid=(groups,),
        in_specs=[fixed(x.shape), w(0), w(1), w(2), b(0), b(1)],
        out_specs=[one] * 4,
        out_shape=[jax.ShapeDtypeStruct(x.shape, BF16)] * 4,
        compiler_params=params(),
        name="temporal_fwd",
    )(x, weight, weight, weight, bias, bias)


def temporal_bwd_body(
    x_ref, q_ref, k_ref, v_ref, g_ref, wq_ref, wk_ref, wv_ref, gain_ref, shift_ref,
    dq_ref, dk_ref, dv_ref, dx_ref, sums_ref, norm_ref, total_ref,
):
    frames, slots, width = x_ref.shape
    rows = frames * STEP
    row = lax.broadcasted_iota(jnp.int32, (rows, rows), 0)
    col = lax.broadcasted_iota(jnp.int32, (rows, rows), 1)
    same = row % STEP == col % STEP
    shape = (frames, STEP, WIDE)
    for step in range(slots // STEP):
        part = slice(step * STEP, (step + 1) * STEP)
        k = k_ref[:, part, :].reshape(rows, WIDE)
        v = v_ref[:, part, :].reshape(rows, WIDE)
        queries = stacked(q_ref[:, part, :].reshape(rows, WIDE), rows)
        grads = stacked(g_ref[:, part, :].reshape(rows, WIDE), rows)
        scores = dot_nt(k, queries)
        grad_mixing = dot_nt(v, grads)
        mixing, grad_scores = [], []
        for head in range(GROUP):
            span = slice(head * rows, (head + 1) * rows)
            s = jnp.where(same, scores[:, span], -1e30)
            e = jnp.exp(s - jnp.max(s, axis=0, keepdims=True))
            p = e / jnp.sum(e, axis=0, keepdims=True)
            gp = grad_mixing[:, span]
            ds = p * (gp - jnp.sum(p * gp, axis=0, keepdims=True))
            mixing.append(p.astype(BF16))
            grad_scores.append(ds.astype(BF16))
        grad_scores = jnp.concatenate(grad_scores, axis=1)
        dv_ref[:, part, :] = dot(jnp.concatenate(mixing, axis=1), grads).astype(BF16).reshape(shape)
        dk_ref[:, part, :] = dot(grad_scores, queries).astype(BF16).reshape(shape)
        spread = dot_tn(grad_scores, k)
        dq = jnp.zeros((rows, WIDE), F32)
        for head in range(GROUP):
            dq = dq + spread[head * rows : (head + 1) * rows] * head_lanes(rows, head, F32)
        dq_ref[:, part, :] = (dq * HEAD_DIM**-0.5).astype(BF16).reshape(shape)
    flat = (frames * slots, WIDE)
    dq, dk, dv = dq_ref[...].reshape(flat), dk_ref[...].reshape(flat), dv_ref[...].reshape(flat)
    sums_ref[...] = jnp.concatenate([column_sum(dq), column_sum(dv), jnp.zeros((6, WIDE), F32)], axis=0)
    update = dot_nt(dq, wq_ref[...]) + dot_nt(dk, wk_ref[...]) + dot_nt(dv, wv_ref[...])
    group = pl.program_id(0)

    @pl.when(group == 0)
    def _():
        total_ref[...] = update

    @pl.when(group > 0)
    def _():
        total_ref[...] += update

    @pl.when(group == pl.num_programs(0) - 1)
    def _():
        total = total_ref[...]
        dx_ref[...] = total.astype(BF16).reshape(frames, slots, width)
        x = x_ref[...].reshape(frames * slots, width).astype(F32)
        shift_grad = column_sum(total)
        gain_grad = (column_sum(total * x) - shift_ref[...] * shift_grad) / gain_ref[...]
        norm_ref[...] = jnp.concatenate([gain_grad, shift_grad, jnp.zeros((6, width), F32)], axis=0)


def temporal_bwd(x, q, k, v, grad, weight, gain, shift):
    frames, slots, width = x.shape
    groups = width // WIDE
    w = lambda part: pl.BlockSpec((width, WIDE), lambda g: (0, part * groups + g))
    one = pl.BlockSpec((frames, slots, WIDE), lambda g: (0, 0, g))
    return pl.pallas_call(
        temporal_bwd_body,
        grid=(groups,),
        in_specs=[fixed(x.shape), one, one, one, one, w(0), w(1), w(2), fixed((1, width)), fixed((1, width))],
        out_specs=[one, one, one, fixed(x.shape), pl.BlockSpec((8, WIDE), lambda g: (0, g)), fixed((8, width))],
        out_shape=[jax.ShapeDtypeStruct(x.shape, BF16)] * 4 + [jax.ShapeDtypeStruct((8, width), F32)] * 2,
        scratch_shapes=[pltpu.VMEM((frames * slots, width), F32)],
        compiler_params=params(),
        name="temporal_bwd",
    )(x, q, k, v, grad, weight, weight, weight, gain, shift)


def middle_body(mixed_ref, video_ref, proj_ref, pb_ref, gain_ref, shift_ref, w_ref, bias_ref, first_ref, normed_ref, qkv_ref):
    slots, width = video_ref.shape
    first = video_ref[...].astype(F32) + (dot(mixed_ref[:slots, :], proj_ref[...]) + pb_ref[...])
    first_ref[...] = first
    unit, _ = norm_parts(first)
    normed_ref[...] = (unit * gain_ref[...] + shift_ref[...]).astype(BF16)
    normed = normed_ref[...]
    q = dot(normed, w_ref[:, :width]) + bias_ref[:, :width]
    qkv_ref[:, :width] = (q * HEAD_DIM**-0.5).astype(BF16)
    qkv_ref[:, width : 2 * width] = dot(normed, w_ref[:, width : 2 * width]).astype(BF16)
    qkv_ref[:, 2 * width :] = (dot(normed, w_ref[:, 2 * width :]) + bias_ref[:, width:]).astype(BF16)


def middle(mixed, video, proj, proj_bias, gain, shift, weight, bias):
    frames, slots, width = video.shape
    per = lambda rows, cols: pl.BlockSpec((None, rows, cols), lambda f: (f, 0, 0))
    return pl.pallas_call(
        middle_body,
        grid=(frames,),
        in_specs=[
            per(mixed.shape[1], width), per(slots, width), fixed(proj.shape), fixed((1, width)), fixed((1, width)),
            fixed((1, width)), fixed(weight.shape), fixed((1, 2 * width)),
        ],
        out_specs=[per(slots, width), per(slots, width), per(slots, 3 * width)],
        out_shape=[
            jax.ShapeDtypeStruct(video.shape, F32),
            jax.ShapeDtypeStruct(video.shape, BF16),
            jax.ShapeDtypeStruct((frames, slots, 3 * width), BF16),
        ],
        compiler_params=params(),
        name="middle",
    )(mixed, video, proj, proj_bias, gain, shift, weight, bias)


def gelu_both(value):
    half = 0.5 * (1.0 + lax.erf(value * 0.7071067811865476))
    density = jnp.exp(-0.5 * value * value) * 0.3989422804014327
    return value * half, half + value * density


def feed_body(
    first_ref, mixed_ref, cot_ref, proj_ref, pb_ref, gain_ref, shift_ref, fc1_ref, fb1_ref, fc2_ref, fb2_ref,
    out_ref, normed_ref, hidden_ref, gi_ref, gs_ref, gso_ref, gspace_ref, sums_ref, unitsum_ref,
    second, branch, gnorm, *, sub,
):
    frame, chunk = pl.program_id(0), pl.program_id(1)
    slots, width = first_ref.shape
    units = fc1_ref.shape[1]

    @pl.when(chunk == 0)
    def _():
        value = first_ref[...] + (dot(mixed_ref[...], proj_ref[...]) + pb_ref[...])
        second[...] = value
        unit, _ = norm_parts(value)
        normed_ref[...] = (unit * gain_ref[...] + shift_ref[...]).astype(BF16)
        branch[...] = jnp.zeros_like(branch)
        gnorm[...] = jnp.zeros_like(gnorm)

    @pl.when(jnp.logical_and(frame == 0, chunk == 0))
    def _():
        sums_ref[...] = jnp.zeros_like(sums_ref)
        unitsum_ref[...] = jnp.zeros_like(unitsum_ref)

    normed = normed_ref[...]
    cot = cot_ref[...]
    for start in range(0, units, sub):
        span = slice(start, start + sub)
        inner = dot(normed, fc1_ref[:, span]) + fb1_ref[0:1, span]
        grad_hidden = dot_nt(cot, fc2_ref[span, :])
        act, slope = gelu_both(inner)
        hidden_ref[:, span] = act.astype(BF16)
        gi_ref[:, span] = (grad_hidden * slope).astype(BF16)
    branch[...] += dot(hidden_ref[...], fc2_ref[...])
    gnorm[...] += dot_nt(gi_ref[...], fc1_ref[...])
    unitsum_ref[chunk, 0:1, :] += column_sum(gi_ref[...])

    @pl.when(chunk == pl.num_programs(1) - 1)
    def _():
        value = second[...]
        out_ref[...] = (value + (branch[...] + fb2_ref[...])).astype(BF16)
        unit, scale = norm_parts(value)
        grad = gnorm[...]
        cot_full = cot_ref[...].astype(F32)
        grad_second = cot_full + norm_grad(grad, unit, scale, gain_ref[...])
        gs_ref[...] = grad_second
        gso_ref[...] = grad_second.astype(BF16)
        gspace_ref[...] = dot_nt(gso_ref[...], proj_ref[...]).astype(BF16)
        sums_ref[0:1, :] += column_sum(grad * unit)
        sums_ref[1:2, :] += column_sum(grad)
        sums_ref[2:3, :] += column_sum(gso_ref[...])
        sums_ref[3:4, :] += column_sum(cot_full)


def feed(first, mixed, cot, proj, proj_bias, gain, shift, fc1, fc1_bias, fc2, fc2_bias, sub=256):
    frames, slots, width = first.shape
    chunks, _, units = fc1.shape
    sub = units if units % sub else sub
    per = pl.BlockSpec((None, slots, width), lambda f, c: (f, 0, 0))
    row = fixed((1, width))
    hid = pl.BlockSpec((None, None, slots, units), lambda f, c: (c, f, 0, 0))
    hid_shape = jax.ShapeDtypeStruct((chunks, frames, slots, units), BF16)
    tok = lambda dtype: jax.ShapeDtypeStruct(first.shape, dtype)
    return pl.pallas_call(
        functools.partial(feed_body, sub=sub),
        grid=(frames, chunks),
        in_specs=[
            per, per, per, fixed(proj.shape), row, row, row,
            pl.BlockSpec((None, width, units), lambda f, c: (c, 0, 0)),
            pl.BlockSpec((None, 1, units), lambda f, c: (c, 0, 0)),
            pl.BlockSpec((None, units, width), lambda f, c: (c, 0, 0)),
            row,
        ],
        out_specs=[per, per, hid, hid, per, per, per, fixed((8, width)), fixed((chunks, 8, units))],
        out_shape=[
            tok(BF16), tok(BF16), hid_shape, hid_shape, tok(F32), tok(BF16), tok(BF16),
            jax.ShapeDtypeStruct((8, width), F32), jax.ShapeDtypeStruct((chunks, 8, units), F32),
        ],
        scratch_shapes=[pltpu.VMEM((slots, width), F32)] * 3,
        compiler_params=params(60),
        name="feed",
    )(first, mixed, cot, proj, proj_bias, gain, shift, fc1, fc1_bias, fc2, fc2_bias)


def middle_bwd_body(
    dq_ref, dk_ref, dv_ref, w_ref, first_ref, gs_ref, gain_ref, proj_ref, gf_ref, gto_ref, gt_ref, sums_ref
):
    slots, width = first_ref.shape
    dq, dk, dv = dq_ref[...], dk_ref[...], dv_ref[...]
    grad = dot_nt(dq, w_ref[:, :width]) + dot_nt(dk, w_ref[:, width : 2 * width]) + dot_nt(dv, w_ref[:, 2 * width :])
    unit, scale = norm_parts(first_ref[...])
    grad_first = gs_ref[...] + norm_grad(grad, unit, scale, gain_ref[...])
    gf_ref[...] = grad_first
    gto_ref[...] = grad_first.astype(BF16)
    gt_ref[:slots, :] = dot_nt(gto_ref[...], proj_ref[...]).astype(BF16)
    if gt_ref.shape[0] > slots:
        gt_ref[slots:, :] = jnp.zeros((gt_ref.shape[0] - slots, width), BF16)

    @pl.when(pl.program_id(0) == 0)
    def _():
        sums_ref[...] = jnp.zeros_like(sums_ref)

    sums_ref[0:1, :] += column_sum(grad * unit)
    sums_ref[1:2, :] += column_sum(grad)
    sums_ref[2:3, :] += column_sum(dq)
    sums_ref[3:4, :] += column_sum(dv)
    sums_ref[4:5, :] += column_sum(gto_ref[...])


def middle_bwd(dq, dk, dv, weight, first, grad_second, gain, proj, padded):
    frames, slots, width = first.shape
    per = lambda rows: pl.BlockSpec((None, rows, width), lambda f: (f, 0, 0))
    return pl.pallas_call(
        middle_bwd_body,
        grid=(frames,),
        in_specs=[
            per(slots), per(slots), per(slots), fixed(weight.shape), per(slots), per(slots), fixed((1, width)), fixed(proj.shape)
        ],
        out_specs=[per(slots), per(slots), per(padded), fixed((8, width))],
        out_shape=[
            jax.ShapeDtypeStruct(first.shape, F32), jax.ShapeDtypeStruct(first.shape, BF16),
            jax.ShapeDtypeStruct((frames, padded, width), BF16), jax.ShapeDtypeStruct((8, width), F32),
        ],
        compiler_params=params(60),
        name="middle_bwd",
    )(dq, dk, dv, weight, first, grad_second, gain, proj)


def norm_out_body(grad_ref, video_ref, gf_ref, gain_ref, out_ref):
    slots = video_ref.shape[0]
    unit, scale = norm_parts(video_ref[...].astype(F32))
    out_ref[...] = gf_ref[...] + norm_grad(grad_ref[:slots, :].astype(F32), unit, scale, gain_ref[...])


def norm_out(grad, video, grad_first, gain):
    frames, slots, width = video.shape
    per = lambda rows: pl.BlockSpec((None, rows, width), lambda f: (f, 0, 0))
    return pl.pallas_call(
        norm_out_body,
        grid=(frames,),
        in_specs=[per(grad.shape[1]), per(slots), per(slots), fixed((1, width))],
        out_specs=per(slots),
        out_shape=jax.ShapeDtypeStruct(video.shape, F32),
        compiler_params=params(),
        name="norm_out",
    )(grad, video, grad_first, gain)


def tn_body(a_ref, b_ref, out_ref):
    out_ref[...] = dot_tn(a_ref[...], b_ref[...]).astype(out_ref.dtype)


def weight_grads(pairs):
    found = []
    for a, many in pairs:
        rows, width = a.shape
        for b in many:
            found.append(
                pl.pallas_call(
                    tn_body,
                    grid=(width // WIDE,),
                    in_specs=[fixed(a.shape), pl.BlockSpec((rows, WIDE), lambda i: (0, i))],
                    out_specs=pl.BlockSpec((width, WIDE), lambda i: (0, i)),
                    out_shape=jax.ShapeDtypeStruct((width, width), BF16),
                    cost_estimate=pl.CostEstimate(
                        flops=2 * rows * width * width, bytes_accessed=4 * rows * width, transcendentals=0
                    ),
                    compiler_params=params(),
                    name="weight_grad",
                )(a, b)
            )
    return jnp.stack(found)


def fc_grads_body(normed_ref, cot_ref, gi_ref, hid_ref, out_ref):
    units = gi_ref.shape[1]
    out_ref[:, :units] = dot_tn(normed_ref[...], gi_ref[...]).astype(BF16)
    out_ref[:, units:] = dot_tn(cot_ref[...], hid_ref[...]).astype(BF16)


def fc_grads(normed, cot, grad_inner, hidden):
    chunks, frames, slots, units = hidden.shape
    width = normed.shape[-1]
    rows = frames * slots
    hid = pl.BlockSpec((None, rows, units), lambda c: (c, 0, 0))
    flat = lambda value: value.reshape(chunks, rows, units)
    return pl.pallas_call(
        fc_grads_body,
        grid=(chunks,),
        in_specs=[fixed((rows, width)), fixed((rows, width)), hid, hid],
        out_specs=pl.BlockSpec((None, width, 2 * units), lambda c: (c, 0, 0)),
        out_shape=jax.ShapeDtypeStruct((chunks, width, 2 * units), BF16),
        cost_estimate=pl.CostEstimate(
            flops=4 * rows * width * units * chunks, bytes_accessed=4 * rows * units * chunks, transcendentals=0
        ),
        compiler_params=params(),
        name="fc_grads",
    )(normed.reshape(rows, width), cot.reshape(rows, width), flat(grad_inner), flat(hidden))


def shards(
    video,
    patch_width,
    temporal_gain,
    temporal_shift,
    temporal_qkv,
    temporal_qv_bias,
    temporal_proj,
    temporal_proj_bias,
    spatial_gain,
    spatial_shift,
    spatial_qkv,
    spatial_qv_bias,
    spatial_proj,
    spatial_proj_bias,
    mlp_gain,
    mlp_shift,
    fc1_weight,
    fc1_bias,
    fc2_weight,
    fc2_bias,
    cotangent,
):
    frames, sets, slots, width = video.shape
    units = fc1_weight.shape[1]
    parts, planes = lax.axis_size("mp"), lax.axis_size("dp")
    share = -(-slots // (parts * STEP)) * STEP
    padded = share * parts
    row = lambda value: value.astype(F32).reshape(1, -1)
    video = video.reshape(frames * sets, slots, width)
    cot = cotangent.reshape(frames * sets, slots, width)

    piece = width // planes
    mine = lax.axis_index("dp") * piece
    own = jnp.concatenate(
        [lax.dynamic_slice_in_dim(fc1_weight, mine, piece, 0), lax.dynamic_slice_in_dim(fc2_weight, mine, piece, 0)], axis=1
    ) if units == width else None
    if own is not None:
        both = lax.all_gather(own, ("mp", "dp"), axis=0, tiled=True).reshape(parts, width, 2 * units)
        fc1, fc2 = both[:, :, :units], both[:, :, units:]
    else:
        piece2 = units // planes
        fc1 = lax.all_gather(lax.dynamic_slice_in_dim(fc1_weight, mine, piece, 0), ("mp", "dp"), axis=0, tiled=True)
        fc1 = fc1.reshape(parts, width, units)
        fc2 = lax.all_gather(
            lax.dynamic_slice_in_dim(fc2_weight, lax.axis_index("dp") * piece2, piece2, 0), ("mp", "dp"), axis=0, tiled=True
        ).reshape(parts, units, width)
    fb1 = lax.all_gather(fc1_bias, "mp", axis=0, tiled=True).astype(F32).reshape(parts, 1, units)

    normed_in = norm_in(video, row(temporal_gain), row(temporal_shift), padded)
    x = lax.all_to_all(normed_in, "mp", split_axis=1, concat_axis=0, tiled=True)
    tq, tk, tv, time_mixed = temporal_fwd(x, temporal_qkv, row(temporal_qv_bias))
    time_back = lax.all_to_all(time_mixed, "mp", split_axis=0, concat_axis=1, tiled=True)

    first, normed_mid, space_qkv = middle(
        time_back, video, temporal_proj, row(temporal_proj_bias), row(spatial_gain), row(spatial_shift), spatial_qkv,
        row(spatial_qv_bias),
    )
    space_mixed, lse = spatial_fwd(patch_width, space_qkv, frames, slots)

    output, normed_out, hidden, grad_inner, grad_second, grad_space_out, grad_space, feed_sums, unit_sums = feed(
        first, space_mixed, cot, spatial_proj, row(spatial_proj_bias), row(mlp_gain), row(mlp_shift), fc1, fb1, fc2,
        row(fc2_bias),
    )
    fc_part = fc_grads(normed_out, cot, grad_inner, hidden)
    fc_part = lax.psum_scatter(fc_part, "dp", scatter_dimension=1, tiled=True)
    fc_part = lax.psum_scatter(fc_part, "mp", scatter_dimension=0, tiled=True)[0].astype(F32)
    fc1_weight_grad = fc_part[:, :units]
    fc2_weight_grad = fc_part[:, units:].T

    dq, dk, dv = spatial_bwd(patch_width, space_qkv, space_mixed, lse, grad_space, frames, slots)
    grad_first, grad_time_out, grad_time, mid_sums = middle_bwd(
        dq, dk, dv, spatial_qkv, first, grad_second, row(spatial_gain), temporal_proj, padded
    )
    flat = lambda value: value.reshape(-1, width)
    early = weight_grads(
        [
            (flat(normed_mid), [flat(dq), flat(dk), flat(dv)]),
            (flat(space_mixed), [flat(grad_space_out)]),
            (flat(time_back[:, :slots]), [flat(grad_time_out)]),
        ]
    )
    early = lax.psum(early, ("dp", "mp"))

    grad_slot = lax.all_to_all(grad_time, "mp", split_axis=1, concat_axis=0, tiled=True)
    gq, gk, gv, grad_x, bias_sums, norm_sums = temporal_bwd(
        x, tq, tk, tv, grad_slot, temporal_qkv, row(temporal_gain), row(temporal_shift)
    )
    grad_in = lax.all_to_all(grad_x, "mp", split_axis=0, concat_axis=1, tiled=True)
    late = weight_grads([(flat(x), [flat(gq), flat(gk), flat(gv)])])
    late = lax.psum(late, ("dp", "mp"))
    video_grad = norm_out(grad_in, video, grad_first, row(temporal_gain))

    small = jnp.concatenate(
        [unit_sums[:, 0, :].reshape(-1, width), feed_sums[:4], mid_sums[:5], bias_sums[:2], norm_sums[:2]], axis=0
    )
    small = lax.psum(small, ("dp", "mp"))
    count = parts * units // width
    fc1_bias_grad = small[:count].reshape(-1)
    (
        mlp_gain_grad, mlp_shift_grad, spatial_proj_bias_grad, fc2_bias_grad,
        spatial_gain_grad, spatial_shift_grad, space_q_sum, space_v_sum, temporal_proj_bias_grad,
        time_q_sum, time_v_sum, temporal_gain_grad, temporal_shift_grad,
    ) = [small[count + i] for i in range(13)]
    wide = lambda parts_: jnp.concatenate([part.astype(F32) for part in parts_], axis=1)
    return (
        output.reshape(frames, sets, slots, width),
        video_grad.reshape(frames, sets, slots, width),
        temporal_gain_grad,
        temporal_shift_grad,
        wide([late[0], late[1], late[2]]),
        jnp.concatenate([time_q_sum, time_v_sum]),
        early[4].astype(F32),
        temporal_proj_bias_grad,
        spatial_gain_grad,
        spatial_shift_grad,
        wide([early[0], early[1], early[2]]),
        jnp.concatenate([space_q_sum, space_v_sum]),
        early[3].astype(F32),
        spatial_proj_bias_grad,
        mlp_gain_grad,
        mlp_shift_grad,
        fc1_weight_grad,
        fc1_bias_grad,
        fc2_weight_grad,
        fc2_bias_grad,
    )


def solution(mesh):
    tokens = P("mp", "dp", None, None)
    return jax.shard_map(
        shards,
        mesh=mesh,
        in_specs=(tokens, P("dp")) + (P(),) * 14 + (P(None, "mp"), P("mp"), P("mp", None), P(), tokens),
        out_specs=(tokens, tokens) + (P(),) * 14 + (P("dp", "mp"), P(), P("mp", "dp"), P()),
        check_vma=False,
    )
```

time: 1850 us -> 811 us (0.44)
  waiting for transfers between devices: 740 us -> 242 us
  local copies, waits for them, and re-layouts: 497 us -> 49.1 us
  matrix products: 322 us -> 0 us
  Pallas kernels: 0 us -> 295 us
  other arithmetic: 157 us -> 32.2 us
  blocking collectives: 53.2 us -> 162 us
  loops' own time: 30.6 us -> 0 us
    dot_general x37 -> x0, matrix products: 307 us -> none  [the longest x1 26.2 us: shards(): jnp.einsum('...d,fd->...f', group_grad, fc2_weight, preferred_element_typ...]
    pallas_call x0 -> x14, Pallas kernels: none -> 295 us  [the longest x1 54.7 us: spatial_bwd(): pl.pallas_call(functools.partial(spatial_bwd_body, slots=slots, rows=rows...]
    all_gather x2 -> x1, waiting for transfers between devices: 279 us -> 0.02 us  [shards(): lax.all_gather(own, ('mp', 'dp'), axis=0, tiled=True)]
    another operation x24 -> x0, local copies, waits for them, and re-layouts: 128 us -> none
    convert_element_type x24 -> x1, local copies, waits for them, and re-layouts: 117 us -> 2.36 us  [shards(): part.astype(F32)]
    reduce_scatter x4 -> x2, waiting for transfers between devices: 114 us -> 18.7 us  [the longest x1 18.6 us: shards(): lax.psum_scatter(fc_part, 'mp', scatter_dimension=0, tiled=True)[0]]
    all_to_all x4, waiting for transfers between devices: 196 us -> 102 us  [the longest x1 73.6 us: shards(): x = lax.all_to_all(normed_in, 'mp', split_axis=1, concat_axis=0, tiled=True)]
    convert_element_type x12 -> x2, other arithmetic: 93.5 us -> 3.79 us  [the longest x1 2.78 us: shards(): early[3].astype(F32)]
  transfers between devices with their start and end apart: 11 -> 8, of which waited for: 8 -> 4; matrix products, arithmetic and copies ran while one was open for 36% -> 8% of each run, Pallas kernels for 0% -> 27%
where the time goes in v1:
time: 811 us; the launch traced here: 814 us
  Pallas kernels  295 us (36%)
  waiting for transfers between devices  242 us (30%)
  blocking collectives  162 us (20%)
  local copies, waits for them, and re-layouts  49.1 us (6%)
  other arithmetic  32.2 us (4%)
  starting transfers between devices  19.1 us (2%)
  between operations  15 us (2%)
    psum x1, waiting for transfers between devices, shards(): late = lax.psum(late, ('dp', 'mp'))  120 us
    psum x1, blocking collectives, shards(): small = lax.psum(small, ('dp', 'mp'))  104 us
    all_to_all x1, waiting for transfers between devices, shards(): x = lax.all_to_all(normed_in, 'mp', split_axis=1, concat_axis=0, tiled=True)  73.6 us
    all_gather x1, blocking collectives, shards(): lax.all_gather(fc1_bias, 'mp', axis=0, tiled=True).astype(F32)  58.3 us
    pallas_call x1, Pallas kernels, spatial_bwd(): pl.pallas_call(functools.partial(spatial_bwd_body, slots=slots, rows=rows...  54.7 us
    pallas_call x1, Pallas kernels, feed(): pl.pallas_call(functools.partial(feed_body, sub=sub), grid=(frames, chunk...  52.7 us
    pallas_call x1, Pallas kernels, spatial_fwd(): pl.pallas_call(functools.partial(spatial_fwd_body, slots=slots, rows=rows...  32.2 us
    pallas_call x1, Pallas kernels, temporal_bwd(): pl.pallas_call(temporal_bwd_body, grid=(groups,), in_specs=[fixed(x.shape...  31.2 us
  transfers between devices with their start and end apart: 8, of which 4 were waited for; matrix products, arithmetic and copies ran while one was open for 8% of the time, Pallas kernels for 27%

profile of v1, /device:TPU:0, one launch (start us, length us, event | category | flops | bytes accessed | tf_op | source)
XLA Modules:
  0.0 814.3 jit_solution(7947101066096891937)
XLA Ops:
  11.6 4.1 norm_in.1
  15.6 5.8 copy.48
  21.5 6.4 all-to-all-start
  28.5 73.6 %all-to-all-done = bf16[2,832,768]{2,0,1:T(2,128)(2,1)S(1)} async-done(((bf16[2,832,768]{2,0,1:T(2,128)(2,1)}), bf16[2,832,768]{2,0,1:T(2,128)(2,1)S(1)}, u32[]{:S(2)}, u32[]{:S(2)}) %all-to-all-start) | async-done | bytes 2555936 | tf_op jit(solution)/shard_map/all_to_all | solution.py:653
  103.9 28.4 %temporal_fwd.1 = (bf16[8,208,768]{2,1,0:T(8,128)(2,1)}, bf16[8,208,768]{2,1,0:T(8,128)(2,1)}, bf16[8,208,768]{2,1,0:T(8,128)(2,1)}, bf16[8,208,768]{2,1,0:T(8,128)(2,1)}) custom-call(bf16[8,208,768]{2,1,0:T(8,128)(2,1)} %bitcast.85, bf16[768,2304]{1,0:T(8,128)(2,1)} %wv_ref.3, bf16[768,2304]{1,0:T(8,128)(2,1)} %wv_ref.3, bf16[768,2304]{1,0:T(8,128)(2,1)} %wv_ref.3, ...), custom_call_target="tpu_custom_call" | custom-call | tf_op jit(solution)/shard_map/temporal_fwd/pallas_call | solution.py:276
  132.4 3.8 all-to-all-start.1
  141.6 58.3 %all-gather = bf16[4,1,768]{2,1,0:T(2,128)(2,1)S(1)} all-gather(bf16[1,1,768]{2,1,0:T(2,128)(2,1)S(1)} %reshape.203), channel_id=1, replica_groups=mesh['dp'=8,'mp'=4] {'mp'}, dimensions={0}, use_global_device_ids=true | all-gather | bytes 7680 | tf_op jit(solution)/shard_map/all_gather | solution.py:650
  202.2 15.1 %middle.1 = (f32[2,784,768]{2,1,0:T(8,128)}, bf16[2,784,768]{2,1,0:T(8,128)(2,1)}, bf16[2,784,2304]{2,1,0:T(8,128)(2,1)}) custom-call(bf16[2,832,768]{2,1,0:T(8,128)(2,1)} %bitcast.90, bf16[2,784,768]{2,1,0:T(8,128)(2,1)} %bitcast.93, bf16[768,768]{1,0:T(8,128)(2,1)} %proj_ref.5, f32[1,768]{1,0:T(1,128)} %reshape.168.pb_ref, f32[1,768]{1,0:T(1,128)} %reshape.169.gain_ref, ...), custom_call_target="tpu_custom_call" | custom-call | tf_op jit(solution)/shard_map/middle/pallas_call | solution.py:380
  217.3 32.2 %spatial_fwd.1 = (bf16[2,784,768]{2,1,0:T(8,128)(2,1)}, f32[2,3,8,784]{3,2,1,0:T(8,128)}) custom-call(s32[1]{0:T(128)S(6)} %copy.63.width_ref, bf16[2,784,2304]{2,1,0:T(8,128)(2,1)} %get-tuple-element.53.q_ref.k_ref.v_ref, bf16[2,784,2304]{2,1,0:T(8,128)(2,1)} %get-tuple-element.53.q_ref.k_ref.v_ref, bf16[2,784,2304]{2,1,0:T(8,128)(2,1)} %get-tuple-element.53.q_ref.k_ref.v_ref), custom_call_target="tpu_custom_call" | custom-call | tf_op jit(solution)/shard_map/spatial_fwd/pallas_call | solution.py:95
  249.5 8.1 fusion.2
  257.7 52.7 %feed.1 = (bf16[2,784,768]{2,1,0:T(8,128)(2,1)}, bf16[2,784,768]{2,1,0:T(8,128)(2,1)}, bf16[4,2,784,768]{3,2,1,0:T(8,128)(2,1)}, bf16[4,2,784,768]{3,2,1,0:T(8,1...) custom-call(f32[2,784,768]{2,1,0:T(8,128)} %get-tuple-element.52.fir, ...), custom_call_target="tpu_custom_call" | custom-call | tf_op jit(solution)/shard_map/feed/pallas_call | solution.py:466
  310.4 23.1 %fc_grads.1 = bf16[4,768,1536]{2,1,0:T(8,128)(2,1)} custom-call(bf16[1568,768]{1,0:T(8,128)(2,1)} %bitcast.124, bf16[1568,768]{1,0:T(8,128)(2,1)} %bitcast.105, bf16[4,1568,768]{2,1,0:T(8,128)(2,1)} %bitcast.114, bf16[4,1568,768]{2,1,0:T(8,128)(2,1)} %bitcast.113), custom_call_target="tpu_custom_call" | custom-call | flops 14797504512 | bytes 19267584 | tf_op jit(solution)/shard_map/fc_grads/pallas_call | solution.py:589
  333.5 54.7 %spatial_bwd.1 = (bf16[2,784,768]{2,1,0:T(8,128)(2,1)}, bf16[2,784,768]{2,1,0:T(8,128)(2,1)}, bf16[2,784,768]{2,1,0:T(8,128)(2,1)}) custom-call(s32[1]{0:T(128)S(6)} %copy.63.width_ref, bf16[2,784,2304]{2,1,0:T(8,128)(2,1)} %get-tuple-element.53.q_ref.k_ref.v_ref, bf16[2,784,2304]{2,1,0:T(8,128)(2,1)} %get-tuple-element.53.q_ref.k_ref.v_ref, ...), custom_call_target="tpu_custom_call" | custom-call | tf_op jit(solution)/shard_map/spatial_bwd/pallas_call | solution.py:174
  388.2 23.0 %middle_bwd.1 = (f32[2,784,768]{2,1,0:T(8,128)}, bf16[2,784,768]{2,1,0:T(8,128)(2,1)}, bf16[2,832,768]{2,1,0:T(8,128)(2,1)}, f32[8,768]{1,0:T(8,128)}) custom-call(bf16[2,784,768]{2,1,0:T(8,128)(2,1)} %get-tuple-element.61.dq_ref, bf16[2,784,768]{2,1,0:T(8,128)(2,1)} %get-tuple-element.62.dk_ref, bf16[2,784,768]{2,1,0:T(8,128)(2,1)} %get-tuple-element.63.dv_ref, ...), custom_call_target="tpu_custom_call" | custom-call | tf_op jit(solution)/shard_map/middle_bwd/pallas_call | solution.py:515
  411.2 5.8 copy.51
  417.0 4.7 all-to-all-start.2
  423.3 6.0 weight_grad.11
  431.7 3.8 weight_grad.15
  435.4 3.7 weight_grad.14
  439.2 5.2 weight_grad.13
  444.4 3.7 weight_grad.12
  448.1 28.5 %all-to-all-done.2 = bf16[2,832,768]{2,0,1:T(2,128)(2,1)} async-done(((bf16[2,832,768]{2,0,1:T(2,128)(2,1)}), bf16[2,832,768]{2,0,1:T(2,128)(2,1)}, u32[]{:S(2)}, u32[]{:S(2)}) %all-to-all-start.2) | async-done | bytes 2555936 | tf_op jit(solution)/shard_map/all_to_all | solution.py:687
  476.7 3.5 copy.52
  480.2 31.2 %temporal_bwd.1 = (bf16[8,208,768]{2,1,0:T(8,128)(2,1)}, bf16[8,208,768]{2,1,0:T(8,128)(2,1)}, bf16[8,208,768]{2,1,0:T(8,128)(2,1)}, bf16[8,208,768]{2,1,0:T(8,1...) custom-call(bf16[8,208,768]{2,1,0:T(8,128)(2,1)} %bitcast.86, bf16[8,208,768]{2,1,0:T(8,128)(2,1)} %get-tuple-element.56.q_ref, ...), custom_call_target="tpu_custom_call" | custom-call | tf_op jit(solution)/shard_map/temporal_bwd/pallas_call | solution.py:352
  511.4 5.9 weight_grad.8
  517.3 5.9 weight_grad.9
  523.2 6.1 weight_grad.10
  532.4 4.0 all-to-all-start.3
  538.9 103.5 %psum.21 = f32[17,768]{1,0:T(8,128)S(1)} all-reduce(f32[17,768]{1,0:T(8,128)S(1)} %concatenate.25), channel_id=1, replica_groups=mesh['dp'=8,'mp'=4] {'dp','mp'}, use_global_device_ids=true, to_apply=%region_0.0 | all-reduce | flops 13056 | bytes 104448 | tf_op jit(solution)/shard_map/psum | solution.py:699
  646.6 7.1 norm_out.1
  653.7 120.4 %all-reduce.3.cloned.1.call-done = (bf16[3,768,768]{2,1,0:T(8,128)(2,1)}, bf16[5,768,768]{2,1,0:T(8,128)(2,1)}) async-done(((bf16[3,768,768]{2,1,0:T(8,128)(2,1)}, bf16[5,768,768]{2,1,0:T(8,128)(2,1)}), (bf16[3,768,768]{2,1,0:T(8,128)(2,1)}, bf16[5,768,768]{2,1,0:T(8,128)(2,1)})) %all-reduce.3.cloned.1.call-update) | async-done | bytes 9437200 | tf_op jit(solution)/shard_map/psum | solution.py:693
  787.0 18.6 %reduce-scatter.5.cloned.1.call-done = bf16[1,96,1536]{2,1,0:T(8,128)(2,1)} async-done(((bf16[4,96,1536]{2,1,0:T(8,128)(2,1)}), bf16[1,96,1536]{2,1,0:T(8,128)(2,1)}) %reduce-scatter.5.cloned.1.call-update) | async-done | bytes 294928 | tf_op jit(solution)/shard_map/reduce_scatter | solution.py:669
  (96 shorter events, 42.3 us)
Async XLA Ops:
  7.2 242.3 %all-gather.3.cloned.1.call-start = ((), (), s32[]{:S(2)}) async-start(), calls=%async_computation.6 | async-start | bytes 9732096 | tf_op jit(solution)/shard_map/all_gather | solution.py:641
  21.4 6.5 copy-start.10
  21.5 80.6 %all-to-all-start = ((bf16[2,832,768]{2,0,1:T(2,128)(2,1)}), bf16[2,832,768]{2,0,1:T(2,128)(2,1)S(1)}, u32[]{:S(2)}, u32[]{:S(2)}) async-start(bf16[2,832,768]{2,0,1:T(2,128)(2,1)} %copy.48), calls=%async_computation | async-start | bytes 5111808 | tf_op jit(solution)/shard_map/all_to_all | solution.py:653
  132.3 4.6 copy-start.13
  132.3 5.2 copy-start.14
  132.3 5.8 copy-start.15
  132.3 6.3 copy-start.16
  132.4 6.9 copy-start.17
  132.4 7.5 copy-start.18
  132.4 8.0 copy-start.20
  132.4 8.0 copy-start.19
  132.4 8.6 %copy-start.11 = (f32[1536]{0:T(1024)S(1)}, f32[1536]{0:T(1024)}, u32[]{:S(2)}) copy-start(f32[1536]{0:T(1024)} %param.32) | copy-start | bytes 18436
  132.4 68.1 %all-to-all-start.1 = ((bf16[8,208,768]{2,1,0:T(8,128)(2,1)}), bf16[8,208,768]{2,1,0:T(8,128)(2,1)S(1)}, u32[]{:S(2)}, u32[]{:S(2)}) async-start(bf16[8,208,768]{2,1,0:T(8,128)(2,1)} %get-tuple-element.51), calls=%async_computation.1 | async-start | bytes 5111808 | tf_op jit(solution)/shard_map/all_to_all | solution.py:655
  136.2 400.3 %reduce-scatter.3.cloned.1.call-start = ((), (), s32[]{:S(2)}) async-start(), calls=%async_computation.7 | async-start | bytes 10616832 | tf_op jit(solution)/shard_map/reduce_scatter | solution.py:668
  417.0 4.7 copy-start
  417.0 59.7 %all-to-all-start.2 = ((bf16[2,832,768]{2,0,1:T(2,128)(2,1)}), bf16[2,832,768]{2,0,1:T(2,128)(2,1)}, u32[]{:S(2)}, u32[]{:S(2)}) async-start(bf16[2,832,768]{2,0,1:T(2,128)(2,1)} %copy.51), calls=%async_computation.2 | async-start | bytes 5111808 | tf_op jit(solution)/shard_map/all_to_all | solution.py:687
  421.7 352.4 %all-reduce.3.cloned.1.call-start = ((), (), s32[]{:S(2)}) async-start(), calls=%async_computation.9 | async-start | bytes 18874368 | tf_op jit(solution)/shard_map/psum | solution.py:693
  423.3 8.4 %copy-start.5 = (bf16[2,784,768]{2,1,0:T(8,128)(2,1)S(1)}, bf16[2,784,768]{2,1,0:T(8,128)(2,1)}, u32[]{:S(2)}) copy-start(bf16[2,784,768]{2,1,0:T(8,128)(2,1)} %get-tuple-element.62.dk_ref) | copy-start | bytes 7225348
  423.3 8.4 %copy-start.21 = (bf16[2,784,768]{2,1,0:T(8,128)(2,1)S(1)}, bf16[2,784,768]{2,1,0:T(8,128)(2,1)}, u32[]{:S(2)}) copy-start(bf16[2,784,768]{2,1,0:T(8,128)(2,1)} %get-tuple-element.76) | copy-start | bytes 7225348
  431.7 3.8 copy-start.4
  435.4 3.7 copy-start.1
  439.2 5.2 copy-start.3
  439.2 5.2 copy-start.22
  523.2 6.1 copy-start.6
  523.2 6.1 copy-start.7
  532.4 4.1 copy-start.8
  532.4 4.6 copy-start.12
  532.4 6.1 copy-start.9
  532.4 112.5 %all-to-all-start.3 = ((bf16[8,208,768]{2,1,0:T(8,128)(2,1)}), bf16[8,208,768]{2,1,0:T(8,128)(2,1)S(1)}, u32[]{:S(2)}, u32[]{:S(2)}) async-start(bf16[8,208,768]{2,1,0:T(8,128)(2,1)} %get-tuple-element.66), calls=%async_computation.3 | async-start | bytes 5111808 | tf_op jit(solution)/shard_map/all_to_all | solution.py:691
  536.4 269.3 %reduce-scatter.5.cloned.1.call-start = ((), (), s32[]{:S(2)}) async-start(), calls=%async_computation.8 | async-start | bytes 1474560 | tf_op jit(solution)/shard_map/reduce_scatter | solution.py:669
  774.1 3.7 copy-start.2
Sparse Core Ops, SparseCore 0:
  11.5 120.8 all-gather.2
  333.7 75.3 reduce-scatter.2
  532.5 241.5 all-reduce.2
  776.4 29.2 reduce-scatter.4

commit v2 on v1

--- a/solution.py
+++ b/solution.py
@@ -213,22 +213,40 @@
     return jnp.sum(value.astype(F32), axis=0, keepdims=True)
 
 
+def by_part(parts, share, width):
+    return pl.BlockSpec((parts, None, share, width), lambda f: (0, f, 0, 0))
+
+
 def norm_in_body(video_ref, gain_ref, shift_ref, out_ref):
     unit, _ = norm_parts(video_ref[...].astype(F32))
-    slots = video_ref.shape[0]
-    out_ref[:slots, :] = (unit * gain_ref[...] + shift_ref[...]).astype(BF16)
-    if out_ref.shape[0] > slots:
-        out_ref[slots:, :] = jnp.zeros((out_ref.shape[0] - slots, out_ref.shape[1]), BF16)
-
-
-def norm_in(video, gain, shift, padded):
+    split_positions(out_ref, (unit * gain_ref[...] + shift_ref[...]).astype(BF16))
+
+
+def split_positions(out_ref, value):
+    parts, share, width = out_ref.shape
+    slots = value.shape[0]
+    for part in range(parts):
+        start = part * share
+        count = min(max(slots - start, 0), share)
+        if count > 0:
+            out_ref[part, :count, :] = value[start : start + count, :]
+        if count < share:
+            out_ref[part, count:, :] = jnp.zeros((share - count, width), value.dtype)
+
+
+def joined_positions(ref, slots):
+    parts, share, width = ref.shape
+    return ref[...].reshape(parts * share, width)[:slots, :]
+
+
+def norm_in(video, gain, shift, parts, share):
     frames, slots, width = video.shape
     return pl.pallas_call(
         norm_in_body,
         grid=(frames,),
         in_specs=[pl.BlockSpec((None, slots, width), lambda f: (f, 0, 0)), fixed((1, width)), fixed((1, width))],
-        out_specs=pl.BlockSpec((None, padded, width), lambda f: (f, 0, 0)),
-        out_shape=jax.ShapeDtypeStruct((frames, padded, width), BF16),
+        out_specs=by_part(parts, share, width),
+        out_shape=jax.ShapeDtypeStruct((parts, frames, share, width), BF16),
         compiler_params=params(),
         name="norm_in",
     )(video, gain, shift)
@@ -363,7 +381,7 @@
 
 def middle_body(mixed_ref, video_ref, proj_ref, pb_ref, gain_ref, shift_ref, w_ref, bias_ref, first_ref, normed_ref, qkv_ref):
     slots, width = video_ref.shape
-    first = video_ref[...].astype(F32) + (dot(mixed_ref[:slots, :], proj_ref[...]) + pb_ref[...])
+    first = video_ref[...].astype(F32) + (dot(joined_positions(mixed_ref, slots), proj_ref[...]) + pb_ref[...])
     first_ref[...] = first
     unit, _ = norm_parts(first)
     normed_ref[...] = (unit * gain_ref[...] + shift_ref[...]).astype(BF16)
@@ -381,7 +399,7 @@
         middle_body,
         grid=(frames,),
         in_specs=[
-            per(mixed.shape[1], width), per(slots, width), fixed(proj.shape), fixed((1, width)), fixed((1, width)),
+            by_part(mixed.shape[0], mixed.shape[2], width), per(slots, width), fixed(proj.shape), fixed((1, width)), fixed((1, width)),
             fixed((1, width)), fixed(weight.shape), fixed((1, 2 * width)),
         ],
         out_specs=[per(slots, width), per(slots, width), per(slots, 3 * width)],
@@ -429,11 +447,11 @@
     for start in range(0, units, sub):
         span = slice(start, start + sub)
         inner = dot(normed, fc1_ref[:, span]) + fb1_ref[0:1, span]
-        grad_hidden = dot_nt(cot, fc2_ref[span, :])
+        grad_hidden = dot(cot, fc2_ref[:, span])
         act, slope = gelu_both(inner)
         hidden_ref[:, span] = act.astype(BF16)
         gi_ref[:, span] = (grad_hidden * slope).astype(BF16)
-    branch[...] += dot(hidden_ref[...], fc2_ref[...])
+    branch[...] += dot_nt(hidden_ref[...], fc2_ref[...])
     gnorm[...] += dot_nt(gi_ref[...], fc1_ref[...])
     unitsum_ref[chunk, 0:1, :] += column_sum(gi_ref[...])
 
@@ -454,10 +472,10 @@
         sums_ref[3:4, :] += column_sum(cot_full)
 
 
-def feed(first, mixed, cot, proj, proj_bias, gain, shift, fc1, fc1_bias, fc2, fc2_bias, sub=256):
+def feed(first, mixed, cot, proj, proj_bias, gain, shift, joint, fc1_bias, fc2_bias, sub=None):
     frames, slots, width = first.shape
-    chunks, _, units = fc1.shape
-    sub = units if units % sub else sub
+    chunks, _, units = fc1_bias.shape
+    sub = sub or units
     per = pl.BlockSpec((None, slots, width), lambda f, c: (f, 0, 0))
     row = fixed((1, width))
     hid = pl.BlockSpec((None, None, slots, units), lambda f, c: (c, f, 0, 0))
@@ -470,7 +488,7 @@
             per, per, per, fixed(proj.shape), row, row, row,
             pl.BlockSpec((None, width, units), lambda f, c: (c, 0, 0)),
             pl.BlockSpec((None, 1, units), lambda f, c: (c, 0, 0)),
-            pl.BlockSpec((None, units, width), lambda f, c: (c, 0, 0)),
+            pl.BlockSpec((None, width, units), lambda f, c: (c, 0, 1)),
             row,
         ],
         out_specs=[per, per, hid, hid, per, per, per, fixed((8, width)), fixed((chunks, 8, units))],
@@ -481,7 +499,7 @@
         scratch_shapes=[pltpu.VMEM((slots, width), F32)] * 3,
         compiler_params=params(60),
         name="feed",
-    )(first, mixed, cot, proj, proj_bias, gain, shift, fc1, fc1_bias, fc2, fc2_bias)
+    )(first, mixed, cot, proj, proj_bias, gain, shift, joint, fc1_bias, joint, fc2_bias)
 
 
 def middle_bwd_body(
@@ -494,9 +512,7 @@
     grad_first = gs_ref[...] + norm_grad(grad, unit, scale, gain_ref[...])
     gf_ref[...] = grad_first
     gto_ref[...] = grad_first.astype(BF16)
-    gt_ref[:slots, :] = dot_nt(gto_ref[...], proj_ref[...]).astype(BF16)
-    if gt_ref.shape[0] > slots:
-        gt_ref[slots:, :] = jnp.zeros((gt_ref.shape[0] - slots, width), BF16)
+    split_positions(gt_ref, dot_nt(gto_ref[...], proj_ref[...]).astype(BF16))
 
     @pl.when(pl.program_id(0) == 0)
     def _():
@@ -509,7 +525,7 @@
     sums_ref[4:5, :] += column_sum(gto_ref[...])
 
 
-def middle_bwd(dq, dk, dv, weight, first, grad_second, gain, proj, padded):
+def middle_bwd(dq, dk, dv, weight, first, grad_second, gain, proj, parts, share):
     frames, slots, width = first.shape
     per = lambda rows: pl.BlockSpec((None, rows, width), lambda f: (f, 0, 0))
     return pl.pallas_call(
@@ -518,10 +534,10 @@
         in_specs=[
             per(slots), per(slots), per(slots), fixed(weight.shape), per(slots), per(slots), fixed((1, width)), fixed(proj.shape)
         ],
-        out_specs=[per(slots), per(slots), per(padded), fixed((8, width))],
+        out_specs=[per(slots), per(slots), by_part(parts, share, width), fixed((8, width))],
         out_shape=[
             jax.ShapeDtypeStruct(first.shape, F32), jax.ShapeDtypeStruct(first.shape, BF16),
-            jax.ShapeDtypeStruct((frames, padded, width), BF16), jax.ShapeDtypeStruct((8, width), F32),
+            jax.ShapeDtypeStruct((parts, frames, share, width), BF16), jax.ShapeDtypeStruct((8, width), F32),
         ],
         compiler_params=params(60),
         name="middle_bwd",
@@ -531,7 +547,7 @@
 def norm_out_body(grad_ref, video_ref, gf_ref, gain_ref, out_ref):
     slots = video_ref.shape[0]
     unit, scale = norm_parts(video_ref[...].astype(F32))
-    out_ref[...] = gf_ref[...] + norm_grad(grad_ref[:slots, :].astype(F32), unit, scale, gain_ref[...])
+    out_ref[...] = gf_ref[...] + norm_grad(joined_positions(grad_ref, slots).astype(F32), unit, scale, gain_ref[...])
 
 
 def norm_out(grad, video, grad_first, gain):
@@ -540,7 +556,7 @@
     return pl.pallas_call(
         norm_out_body,
         grid=(frames,),
-        in_specs=[per(grad.shape[1]), per(slots), per(slots), fixed((1, width))],
+        in_specs=[by_part(grad.shape[0], grad.shape[2], width), per(slots), per(slots), fixed((1, width))],
         out_specs=per(slots),
         out_shape=jax.ShapeDtypeStruct(video.shape, F32),
         compiler_params=params(),
@@ -598,6 +614,207 @@
         compiler_params=params(),
         name="fc_grads",
     )(normed.reshape(rows, width), cot.reshape(rows, width), flat(grad_inner), flat(hidden))
+
+
+MESH = pl.DeviceIdType.MESH
+
+
+def bits_of(count):
+    return [1 << i for i in range(count.bit_length() - 1)]
+
+
+def reducible(width, planes, parts):
+    power = planes >= 4 and planes & (planes - 1) == 0 and parts & (parts - 1) == 0
+    return power and width % (planes * 2 * 16) == 0
+
+
+def reduce_body(*refs, counts, planes, parts, has_small):
+    total = sum(counts)
+    inputs, refs = refs[: len(counts) + total], refs[len(counts) + total :]
+    if has_small:
+        small_ref, refs = refs[0], refs[1:]
+    out_ref, refs = refs[0], refs[1:]
+    if has_small:
+        small_out, refs = refs[0], refs[1:]
+    own, final = refs[:2]
+    bits, hops = bits_of(planes), bits_of(parts)
+    deep, steps = len(bits), len(bits) + len(hops)
+    got = refs[2 : 2 + steps]
+    held = refs[2 + steps : 1 + 2 * steps]
+    refs = refs[1 + 2 * steps :]
+    send_sem, recv_sem, out_sem = refs[:3]
+    if has_small:
+        small_got, small_held, small_send, small_recv = refs[3:7]
+    plane, part = lax.axis_index("dp"), lax.axis_index("mp")
+    place = lambda bit: (plane // bit) % 2
+    swap_plane = lambda bit: {"dp": plane + bit - 2 * bit * place(bit)}
+    swap_part = lambda bit: {"mp": part + bit - 2 * bit * ((part // bit) % 2)}
+    partners = [swap_plane(bit) for bit in bits] + [swap_part(bit) for bit in hops]
+
+    barrier = pltpu.get_barrier_semaphore()
+    for partner in partners:
+        pl.semaphore_signal(barrier, inc=1, device_id=partner, device_id_type=MESH)
+    pl.semaphore_wait(barrier, len(partners))
+
+    width = own.shape[1]
+    started = []
+    waiting = {}
+
+    def send(chain, step, source, target, partner):
+        copy = pltpu.make_async_remote_copy(
+            src_ref=source, dst_ref=target, send_sem=send_sem.at[chain, step], recv_sem=recv_sem.at[chain, step],
+            device_id=partner, device_id_type=MESH,
+        )
+        copy.start()
+        started.append(copy)
+        waiting[chain] = copy
+
+    def order(stream):
+        return bits if stream == 0 else bits[:1] + bits[1:][::-1]
+
+    def rows_at(offset, size):
+        return pl.ds(pl.multiple_of(offset, 16), size)
+
+    def advance(chain, step):
+        matrix, stream = chain // 2, chain % 2
+        mine = order(stream)
+        size = width // 2
+        if step > 0:
+            waiting[chain].wait_recv()
+        if step == 0:
+            half = (1 - place(mine[0])) * size + stream * (size // 2)
+            send(chain, 0, own.at[matrix, rows_at(half, size // 2)], got[0].at[chain], partners_of[mine[0]])
+            return
+        if step <= steps:
+            before = step - 1
+            count = got[before].shape[1]
+            if before == 0:
+                kept = own[matrix, rows_at(place(mine[0]) * size + stream * (size // 2), count), :]
+            elif before < deep:
+                kept = held[before - 1][chain, rows_at(place(mine[before]) * count, count), :]
+            else:
+                kept = held[before - 1][chain]
+            value = (kept.astype(F32) + got[before][chain].astype(F32)).astype(BF16)
+            if step < steps:
+                held[before][chain] = value
+                if step < deep:
+                    half = count // 2
+                    source = held[before].at[chain, rows_at((1 - place(mine[step])) * half, half)]
+                    send(chain, step, source, got[step].at[chain], partners_of[mine[step]])
+                else:
+                    send(chain, step, held[before].at[chain], got[step].at[chain], swap_part(hops[step - deep]))
+                return
+            spot, length = offsets(chain, deep)
+            final[matrix, rows_at(spot, length), :] = value
+        back = step - steps
+        if back < deep:
+            level = deep - back
+            spot, length = offsets(chain, level)
+            region = final.at[matrix, rows_at(spot, length)]
+            send(chain, step, region, region, partners_of[mine[level - 1]])
+        elif stream == 1:
+            write = pltpu.make_async_copy(final.at[matrix], out_ref.at[matrix], out_sem.at[matrix])
+            write.start()
+            written.append(write)
+
+    def offsets(chain, level):
+        stream = chain % 2
+        mine = order(stream)
+        size = width // 2
+        spot, length = place(mine[0]) * size + stream * (size // 2), size // 2
+        for bit in mine[1:level]:
+            length //= 2
+            spot = spot + place(bit) * length
+        return spot, length
+
+    partners_of = {bit: swap_plane(bit) for bit in bits}
+    written = []
+    pairs = []
+    at = len(counts)
+    for which, count in enumerate(counts):
+        for _ in range(count):
+            pairs.append((inputs[which], inputs[at]))
+            at += 1
+
+    def small_step(step):
+        if step > 0:
+            small_wait.pop().wait_recv()
+            before = small_ref[...] if step == 1 else small_held[step - 2]
+            value = before + small_got[step - 1]
+            if step == steps:
+                small_out[...] = value
+                return
+            small_held[step - 1] = value
+        source = small_ref if step == 0 else small_held.at[step - 1]
+        copy = pltpu.make_async_remote_copy(
+            src_ref=source, dst_ref=small_got.at[step], send_sem=small_send.at[step], recv_sem=small_recv.at[step],
+            device_id=partners[step], device_id_type=MESH,
+        )
+        copy.start()
+        started.append(copy)
+        small_wait.append(copy)
+
+    small_wait = []
+    last = steps + deep
+    for tick in range(total + last):
+        if tick < total:
+            a_ref, b_ref = pairs[tick]
+            own[tick] = dot_tn(a_ref[...], b_ref[...]).astype(BF16)
+        for matrix in range(total):
+            step = tick - matrix
+            if 0 <= step <= last:
+                advance(2 * matrix, step)
+                advance(2 * matrix + 1, step)
+        if has_small and tick <= steps:
+            small_step(tick)
+    for copy in started:
+        copy.wait_send()
+    for write in written:
+        write.wait()
+
+
+def reduced_weight_grads(pairs, small, number):
+    planes, parts = lax.axis_size("dp"), lax.axis_size("mp")
+    width = pairs[0][0].shape[1]
+    counts = [len(many) for _, many in pairs]
+    total = sum(counts)
+    if not reducible(width, planes, parts):
+        grads = lax.psum(weight_grads(pairs), ("dp", "mp"))
+        return (grads,) if small is None else (grads, lax.psum(small, ("dp", "mp")))
+    deep, hops = len(bits_of(planes)), len(bits_of(parts))
+    steps = deep + hops
+    sizes = [width // 4 // (1 << i) for i in range(deep)] + [width // 4 // (1 << (deep - 1))] * hops
+    chains = 2 * total
+    buffers = lambda sizes: [pltpu.VMEM((chains, size, width), BF16) for size in sizes]
+    operands = [a for a, _ in pairs] + [b for _, many in pairs for b in many]
+    whole = pl.BlockSpec(memory_space=pltpu.VMEM)
+    out_shape = [jax.ShapeDtypeStruct((total, width, width), BF16)]
+    out_specs = [pl.BlockSpec(memory_space=pl.ANY)]
+    scratch = (
+        [pltpu.VMEM((total, width, width), BF16)] * 2 + buffers(sizes) + buffers(sizes[:-1])
+        + [pltpu.SemaphoreType.DMA((chains, steps + deep))] * 2 + [pltpu.SemaphoreType.DMA((total,))]
+    )
+    if small is not None:
+        operands.append(small)
+        out_shape.append(jax.ShapeDtypeStruct(small.shape, F32))
+        out_specs.append(whole)
+        scratch += [pltpu.VMEM((steps,) + small.shape, F32), pltpu.VMEM((steps - 1,) + small.shape, F32)]
+        scratch += [pltpu.SemaphoreType.DMA((steps,))] * 2
+    rows = pairs[0][0].shape[0]
+    return pl.pallas_call(
+        functools.partial(reduce_body, counts=counts, planes=planes, parts=parts, has_small=small is not None),
+        in_specs=[whole] * len(operands),
+        out_specs=out_specs,
+        out_shape=out_shape,
+        scratch_shapes=scratch,
+        cost_estimate=pl.CostEstimate(
+            flops=2 * rows * width * width * total * 8, bytes_accessed=4 * rows * width * total * 8, transcendentals=0
+        ),
+        compiler_params=pltpu.CompilerParams(
+            vmem_limit_bytes=60 * MIB, collective_id=number, has_side_effects=True
+        ),
+        name="reduced_weight_grads",
+    )(*operands)
 
 
 def shards(
@@ -627,32 +844,30 @@
     units = fc1_weight.shape[1]
     parts, planes = lax.axis_size("mp"), lax.axis_size("dp")
     share = -(-slots // (parts * STEP)) * STEP
-    padded = share * parts
     row = lambda value: value.astype(F32).reshape(1, -1)
     video = video.reshape(frames * sets, slots, width)
     cot = cotangent.reshape(frames * sets, slots, width)
 
+    joint = jnp.concatenate([fc1_weight, fc2_weight.T], axis=1)
     piece = width // planes
-    mine = lax.axis_index("dp") * piece
-    own = jnp.concatenate(
-        [lax.dynamic_slice_in_dim(fc1_weight, mine, piece, 0), lax.dynamic_slice_in_dim(fc2_weight, mine, piece, 0)], axis=1
-    ) if units == width else None
-    if own is not None:
-        both = lax.all_gather(own, ("mp", "dp"), axis=0, tiled=True).reshape(parts, width, 2 * units)
-        fc1, fc2 = both[:, :, :units], both[:, :, units:]
-    else:
-        piece2 = units // planes
-        fc1 = lax.all_gather(lax.dynamic_slice_in_dim(fc1_weight, mine, piece, 0), ("mp", "dp"), axis=0, tiled=True)
-        fc1 = fc1.reshape(parts, width, units)
-        fc2 = lax.all_gather(
-            lax.dynamic_slice_in_dim(fc2_weight, lax.axis_index("dp") * piece2, piece2, 0), ("mp", "dp"), axis=0, tiled=True
-        ).reshape(parts, units, width)
-    fb1 = lax.all_gather(fc1_bias, "mp", axis=0, tiled=True).astype(F32).reshape(parts, 1, units)
-
-    normed_in = norm_in(video, row(temporal_gain), row(temporal_shift), padded)
-    x = lax.all_to_all(normed_in, "mp", split_axis=1, concat_axis=0, tiled=True)
+    own = lax.dynamic_slice_in_dim(joint, lax.axis_index("dp") * piece, piece, 0)
+    bias_rows = jnp.pad(fc1_bias.reshape(1, units), ((0, 15), (0, units)))
+    own = jnp.concatenate([own, bias_rows], axis=0)[None]
+
+    def exchange(value):
+        return lax.all_to_all(value, "mp", split_axis=0, concat_axis=0, tiled=True)
+
+    by_position = lambda value: value.reshape(parts * frames, share, width)
+    by_device = lambda value: value.reshape(parts, frames, share, width)
+    normed_in = norm_in(video, row(temporal_gain), row(temporal_shift), parts, share)
+    x = by_position(exchange(normed_in))
+    own, x = lax.optimization_barrier((own, x))
+    column = lax.all_gather(own, "mp", axis=0, tiled=True)
     tq, tk, tv, time_mixed = temporal_fwd(x, temporal_qkv, row(temporal_qv_bias))
-    time_back = lax.all_to_all(time_mixed, "mp", split_axis=0, concat_axis=1, tiled=True)
+    column, time_mixed = lax.optimization_barrier((column, time_mixed))
+    fb1 = column[:, piece : piece + 1, :units].astype(F32)
+    joint = lax.all_gather(column[:, :piece], "dp", axis=1, tiled=True)
+    time_back = exchange(by_device(time_mixed))
 
     first, normed_mid, space_qkv = middle(
         time_back, video, temporal_proj, row(temporal_proj_bias), row(spatial_gain), row(spatial_shift), spatial_qkv,
@@ -661,7 +876,7 @@
     space_mixed, lse = spatial_fwd(patch_width, space_qkv, frames, slots)
 
     output, normed_out, hidden, grad_inner, grad_second, grad_space_out, grad_space, feed_sums, unit_sums = feed(
-        first, space_mixed, cot, spatial_proj, row(spatial_proj_bias), row(mlp_gain), row(mlp_shift), fc1, fb1, fc2,
+        first, space_mixed, cot, spatial_proj, row(spatial_proj_bias), row(mlp_gain), row(mlp_shift), joint, fb1,
         row(fc2_bias),
     )
     fc_part = fc_grads(normed_out, cot, grad_inner, hidden)
@@ -672,31 +887,31 @@
 
     dq, dk, dv = spatial_bwd(patch_width, space_qkv, space_mixed, lse, grad_space, frames, slots)
     grad_first, grad_time_out, grad_time, mid_sums = middle_bwd(
-        dq, dk, dv, spatial_qkv, first, grad_second, row(spatial_gain), temporal_proj, padded
+        dq, dk, dv, spatial_qkv, first, grad_second, row(spatial_gain), temporal_proj, parts, share
     )
     flat = lambda value: value.reshape(-1, width)
-    early = weight_grads(
+    grad_slot = exchange(grad_time)
+    time_rows = jnp.swapaxes(time_back, 0, 1).reshape(frames, parts * share, width)[:, :slots]
+    (early,) = reduced_weight_grads(
         [
             (flat(normed_mid), [flat(dq), flat(dk), flat(dv)]),
             (flat(space_mixed), [flat(grad_space_out)]),
-            (flat(time_back[:, :slots]), [flat(grad_time_out)]),
-        ]
+            (flat(time_rows), [flat(grad_time_out)]),
+        ],
+        None,
+        1,
     )
-    early = lax.psum(early, ("dp", "mp"))
-
-    grad_slot = lax.all_to_all(grad_time, "mp", split_axis=1, concat_axis=0, tiled=True)
+
     gq, gk, gv, grad_x, bias_sums, norm_sums = temporal_bwd(
-        x, tq, tk, tv, grad_slot, temporal_qkv, row(temporal_gain), row(temporal_shift)
+        x, tq, tk, tv, by_position(grad_slot), temporal_qkv, row(temporal_gain), row(temporal_shift)
     )
-    grad_in = lax.all_to_all(grad_x, "mp", split_axis=0, concat_axis=1, tiled=True)
-    late = weight_grads([(flat(x), [flat(gq), flat(gk), flat(gv)])])
-    late = lax.psum(late, ("dp", "mp"))
-    video_grad = norm_out(grad_in, video, grad_first, row(temporal_gain))
-
+    grad_in = exchange(by_device(grad_x))
     small = jnp.concatenate(
         [unit_sums[:, 0, :].reshape(-1, width), feed_sums[:4], mid_sums[:5], bias_sums[:2], norm_sums[:2]], axis=0
     )
-    small = lax.psum(small, ("dp", "mp"))
+    small = jnp.pad(small, ((0, -small.shape[0] % 8), (0, 0)))
+    late, small = reduced_weight_grads([(flat(x), [flat(gq), flat(gk), flat(gv)])], small, 2)
+    video_grad = norm_out(grad_in, video, grad_first, row(temporal_gain))
     count = parts * units // width
     fc1_bias_grad = small[:count].reshape(-1)
     (

time: 811 us -> 660 us (0.81); the launches traced: 814 us -> 652 us
  Pallas kernels: 295 us -> 464 us
  blocking collectives: 162 us -> 0 us
  waiting for transfers between devices: 242 us -> 108 us
  local copies, waits for them, and re-layouts: 49.1 us -> 30.8 us
  other arithmetic: 32.2 us -> 16.6 us
    pallas_call x6 -> x4, Pallas kernels: 46.1 us -> 218 us  [the longest x2 196 us: reduced_weight_grads(): pl.pallas_call(functools.partial(reduce_body, counts=counts, planes=plane...]
    psum x1 -> x0, waiting for transfers between devices: 120 us -> none  [shards(): late = lax.psum(late, ('dp', 'mp'))]
    psum x1 -> x0, blocking collectives: 104 us -> none  [shards(): small = lax.psum(small, ('dp', 'mp'))]
    all_gather x1 -> x0, blocking collectives: 58.3 us -> none  [shards(): lax.all_gather(fc1_bias, 'mp', axis=0, tiled=True).astype(F32)]
    reduce_scatter x1, waiting for transfers between devices: 18.6 us -> 0.01 us  [shards(): lax.psum_scatter(fc_part, 'mp', scatter_dimension=0, tiled=True)[0]]
    pallas_call x4 -> x0, other arithmetic: 16.4 us -> none  [weight_grads(): pl.pallas_call(tn_body, grid=(width // WIDE,), in_specs=[fixed(a.shape),...]
    pallas_call x2 -> x0, local copies, waits for them, and re-layouts: 11.6 us -> none  [the longest x1 5.82 us: norm_in(): pl.pallas_call(norm_in_body, grid=(frames,), in_specs=[pl.BlockSpec((None...]
    all_to_all x4 -> x0, local copies, waits for them, and re-layouts: 8.64 us -> none  [the longest x1 3.51 us: shards(): lax.all_to_all(grad_time, 'mp', split_axis=1, concat_axis=0, tiled=True)]
  transfers between devices with their start and end apart: 8 -> 8, of which waited for: 4 -> 3; matrix products, arithmetic and copies ran while one was open for 8% -> 5% of each run, Pallas kernels for 27% -> 59%
where the time goes in v2:
time: 660 us; the launch traced here: 652 us
  Pallas kernels  464 us (70%)
  waiting for transfers between devices  108 us (16%)
  local copies, waits for them, and re-layouts  30.8 us (5%)
  starting transfers between devices  18.5 us (3%)
  other arithmetic  16.6 us (3%)
  between operations  14.9 us (2%)
    pallas_call x2, Pallas kernels, reduced_weight_grads(): pl.pallas_call(functools.partial(reduce_body, counts=counts, planes=plane...  196 us
    all_to_all x4, waiting for transfers between devices, exchange(): return lax.all_to_all(value, 'mp', split_axis=0, concat_axis=0, tiled=True)  104 us
    pallas_call x1, Pallas kernels, spatial_bwd(): pl.pallas_call(functools.partial(spatial_bwd_body, slots=slots, rows=rows...  54.7 us
    pallas_call x1, Pallas kernels, feed(): pl.pallas_call(functools.partial(feed_body, sub=sub), grid=(frames, chunk...  50.3 us
    pallas_call x1, Pallas kernels, spatial_fwd(): pl.pallas_call(functools.partial(spatial_fwd_body, slots=slots, rows=rows...  31.8 us
    pallas_call x1, Pallas kernels, temporal_bwd(): pl.pallas_call(temporal_bwd_body, grid=(groups,), in_specs=[fixed(x.shape...  31.4 us
    pallas_call x1, Pallas kernels, temporal_fwd(): pl.pallas_call(temporal_fwd_body, grid=(groups,), in_specs=[fixed(x.shape...  28.3 us
    pallas_call x1, Pallas kernels, fc_grads(): pl.pallas_call(fc_grads_body, grid=(chunks,), in_specs=[fixed((rows, widt...  23.1 us
  transfers between devices with their start and end apart: 8, of which 3 were waited for; matrix products, arithmetic and copies ran while one was open for 5% of the time, Pallas kernels for 59%

profile of v2, /device:TPU:0, one launch (start us, length us, event | category | flops | bytes accessed | tf_op | source)
XLA Modules:
  0.0 652.0 jit_solution(16682662504169570285)
XLA Ops:
  7.2 1.3 reshape.175.gain_ref
  9.7 4.1 norm_in.1
  13.8 6.4 all-to-all-start
  20.3 2.4 copy.50
  24.4 53.9 %all-to-all-done = bf16[4,2,208,768]{3,2,1,0:T(8,128)(2,1)S(1)} async-done(((bf16[4,2,208,768]{3,2,1,0:T(8,128)(2,1)}), bf16[4,2,208,768]{3,2,1,0:T(8,128)(2,1)S(1)}, u32[]{:S(2)}, u32[]{:S(2)}) %all-to-all-start) | async-done | bytes 2555936 | tf_op jit(solution)/shard_map/all_to_all | solution.py:858
  79.8 28.3 %temporal_fwd.1 = (bf16[8,208,768]{2,1,0:T(8,128)(2,1)}, bf16[8,208,768]{2,1,0:T(8,128)(2,1)}, bf16[8,208,768]{2,1,0:T(8,128)(2,1)}, bf16[8,208,768]{2,1,0:T(8,128)(2,1)}) custom-call(bf16[8,208,768]{2,1,0:T(8,128)(2,1)} %bitcast.59, bf16[768,2304]{1,0:T(8,128)(2,1)} %wv_ref.3, bf16[768,2304]{1,0:T(8,128)(2,1)} %wv_ref.3, bf16[768,2304]{1,0:T(8,128)(2,1)} %wv_ref.3, ...), custom_call_target="tpu_custom_call" | custom-call | tf_op jit(solution)/shard_map/temporal_fwd/pallas_call | solution.py:294
  108.1 3.3 all-gather.3.cloned.1.call-done
  111.4 2.4 slice.96
  113.9 3.8 all-to-all-start.1
  123.5 1.4 slice_convert_fusion.fb1_ref
  125.0 50.3 %all-to-all-done.1.mixed_ref = bf16[4,2,208,768]{3,2,1,0:T(8,128)(2,1)S(1)} async-done(((bf16[4,2,208,768]{3,2,1,0:T(8,128)(2,1)}), bf16[4,2,208,768]{3,2,1,0:T(8,128)(2,1)S(1)}, u32[]{:S(2)}, u32[]{:S(2)}) %all-to-all-start.1) | async-done | bytes 2555936 | tf_op jit(solution)/shard_map/all_to_all | solution.py:858
  175.3 1.5 copy-done.1
  176.7 14.9 %middle.1 = (f32[2,784,768]{2,1,0:T(8,128)}, bf16[2,784,768]{2,1,0:T(8,128)(2,1)}, bf16[2,784,2304]{2,1,0:T(8,128)(2,1)}) custom-call(bf16[4,2,208,768]{3,2,1,0:T(8,128)(2,1)} %copy-done.1, bf16[2,784,768]{2,1,0:T(8,128)(2,1)} %bitcast.64, bf16[768,768]{1,0:T(8,128)(2,1)} %proj_ref.5, f32[1,768]{1,0:T(1,128)} %reshape.180.pb_ref, ...), custom_call_target="tpu_custom_call" | custom-call | tf_op jit(solution)/shard_map/middle/pallas_call | solution.py:398
  191.6 31.8 %spatial_fwd.1 = (bf16[2,784,768]{2,1,0:T(8,128)(2,1)}, f32[2,3,8,784]{3,2,1,0:T(8,128)}) custom-call(s32[1]{0:T(128)S(6)} %copy.55.width_ref, bf16[2,784,2304]{2,1,0:T(8,128)(2,1)} %get-tuple-element.62.q_ref.k_ref.v_ref, bf16[2,784,2304]{2,1,0:T(8,128)(2,1)} %get-tuple-element.62.q_ref.k_ref.v_ref, bf16[2,784,2304]{2,1,0:T(8,128)(2,1)} %get-tuple-element.62.q_ref.k_ref.v_ref), custom_call_target="tpu_custom_call" | custom-call | tf_op jit(solution)/shard_map/spatial_fwd/pallas_call | solution.py:95
  223.4 50.3 %feed.1 = (bf16[2,784,768]{2,1,0:T(8,128)(2,1)}, bf16[2,784,768]{2,1,0:T(8,128)(2,1)}, bf16[4,2,784,768]{3,2,1,0:T(8,128)(2,1)}, bf16[4,2,784,768]{3,2,1,0:T(8,1...) custom-call(f32[2,784,768]{2,1,0:T(8,128)} %get-tuple-element.61.fir, ...), custom_call_target="tpu_custom_call" | custom-call | tf_op jit(solution)/shard_map/feed/pallas_call | solution.py:484
  273.7 23.1 %fc_grads.1 = bf16[4,768,1536]{2,1,0:T(8,128)(2,1)} custom-call(bf16[1568,768]{1,0:T(8,128)(2,1)} %bitcast.89, bf16[1568,768]{1,0:T(8,128)(2,1)} %bitcast.78, bf16[4,1568,768]{2,1,0:T(8,128)(2,1)} %bitcast.81, bf16[4,1568,768]{2,1,0:T(8,128)(2,1)} %bitcast.80), custom_call_target="tpu_custom_call" | custom-call | flops 14797504512 | bytes 19267584 | tf_op jit(solution)/shard_map/fc_grads/pallas_call | solution.py:605
  296.8 1.7 copy-done.2
  298.7 1.6 slice.129
  300.3 54.7 %spatial_bwd.1 = (bf16[2,784,768]{2,1,0:T(8,128)(2,1)}, bf16[2,784,768]{2,1,0:T(8,128)(2,1)}, bf16[2,784,768]{2,1,0:T(8,128)(2,1)}) custom-call(s32[1]{0:T(128)S(6)} %copy.55.width_ref, bf16[2,784,2304]{2,1,0:T(8,128)(2,1)} %get-tuple-element.62.q_ref.k_ref.v_ref, bf16[2,784,2304]{2,1,0:T(8,128)(2,1)} %get-tuple-element.62.q_ref.k_ref.v_ref, ...), custom_call_target="tpu_custom_call" | custom-call | tf_op jit(solution)/shard_map/spatial_bwd/pallas_call | solution.py:174
  355.0 22.2 %middle_bwd.1 = (f32[2,784,768]{2,1,0:T(8,128)}, bf16[2,784,768]{2,1,0:T(8,128)(2,1)}, bf16[4,2,208,768]{3,2,1,0:T(8,128)(2,1)}, f32[8,768]{1,0:T(8,128)}) custom-call(bf16[2,784,768]{2,1,0:T(8,128)(2,1)} %get-tuple-element.71.dq_ref, bf16[2,784,768]{2,1,0:T(8,128)(2,1)} %get-tuple-element.72.dk_ref, bf16[2,784,768]{2,1,0:T(8,128)(2,1)} %get-tuple-element.73.dv_ref, ...), custom_call_target="tpu_custom_call" | custom-call | tf_op jit(solution)/shard_map/middle_bwd/pallas_call | solution.py:531
  377.2 3.9 all-to-all-start.2
  381.1 84.5 %reduced_weight_grads.3 = bf16[5,768,768]{2,1,0:T(8,128)(2,1)} custom-call(bf16[1568,768]{1,0:T(8,128)(2,1)} %bitcast.86, bf16[1568,768]{1,0:T(8,128)(2,1)} %bitcast.68, bf16[1568,768]{1,0:T(8,128)(2,1)} %bitcast.73, bf16[1568,768]{1,0:T(8,128)(2,1)} %bitcast.74, bf16[1568,768]{1,0:T(8,128)(2,1)} %bitcast.75, bf16[1568,768]{1,0:T(8,128)(2,1)} %bitcast.76, ...), custom_call_target="tpu_custom_call" | custom-call | flops 73987522560 | bytes 192675840 | tf_op jit(solution)/shard_map/reduced_weight_grads/pallas_call | solution.py:804
  465.7 6.1 bitcast_convert_fusion
  471.7 1.5 copy-done.4
  473.2 31.4 %temporal_bwd.1 = (bf16[8,208,768]{2,1,0:T(8,128)(2,1)}, bf16[8,208,768]{2,1,0:T(8,128)(2,1)}, bf16[8,208,768]{2,1,0:T(8,128)(2,1)}, bf16[8,208,768]{2,1,0:T(8,1...) custom-call(bf16[8,208,768]{2,1,0:T(8,128)(2,1)} %bitcast.60, bf16[8,208,768]{2,1,0:T(8,128)(2,1)} %get-tuple-element.66.q_ref, ...), custom_call_target="tpu_custom_call" | custom-call | tf_op jit(solution)/shard_map/temporal_bwd/pallas_call | solution.py:370
  506.1 3.8 all-to-all-start.3
  511.0 111.3 %reduced_weight_grads.2 = (bf16[3,768,768]{2,1,0:T(8,128)(2,1)}, f32[24,768]{1,0:T(8,128)}) custom-call(bf16[1664,768]{1,0:T(8,128)(2,1)} %bitcast.61, bf16[1664,768]{1,0:T(8,128)(2,1)} %bitcast.82, bf16[1664,768]{1,0:T(8,128)(2,1)} %bitcast.83, bf16[1664,768]{1,0:T(8,128)(2,1)} %bitcast.84, f32[24,768]{1,0:T(8,128)} %pad.9.refs_4_), custom_call_target="tpu_custom_call" | custom-call | flops 47110422528 | bytes 122683392 | tf_op jit(solution)/shard_map/reduced_weight_grads/pallas_call | solution.py:804
  623.6 1.8 slice_reduce_fusion
  626.1 2.4 slice_bitcast_fusion.5
  629.1 5.7 maximum_convert_fusion
  634.8 1.5 copy-done.3
  636.3 7.1 %norm_out.1 = f32[2,784,768]{2,1,0:T(8,128)} custom-call(bf16[4,2,208,768]{3,2,1,0:T(8,128)(2,1)} %copy-done.3, bf16[2,784,768]{2,1,0:T(8,128)(2,1)} %bitcast.65, f32[2,784,768]{2,1,0:T(8,128)} %get-tuple-element.77.gf_ref, f32[1,768]{1,0:T(1,128)} %reshape.175.gain_ref), custom_call_target="tpu_custom_call" | custom-call | tf_op jit(solution)/shard_map/norm_out/pallas_call | solution.py:556
  (77 shorter events, 17.0 us)
Async XLA Ops:
  13.8 6.5 copy-start.20
  13.8 64.5 %all-to-all-start = ((bf16[4,2,208,768]{3,2,1,0:T(8,128)(2,1)}), bf16[4,2,208,768]{3,2,1,0:T(8,128)(2,1)S(1)}, u32[]{:S(2)}, u32[]{:S(2)}) async-start(bf16[4,2,208,768]{3,2,1,0:T(8,128)(2,1)} %norm_in.1), calls=%async_computation | async-start | bytes 5111808 | tf_op jit(solution)/shard_map/all_to_all | solution.py:858
  20.3 91.1 %all-gather.3.cloned.1.call-start = ((), (), s32[]{:S(2)}) async-start(), calls=%async_computation.6 | async-start | bytes 1720320 | tf_op jit(solution)/shard_map/all_gather | solution.py:865
  20.3 58.1 %copy-start.10 = (f32[1536]{0:T(1024)S(1)}, f32[1536]{0:T(1024)}, u32[]{:S(2)}) copy-start(f32[1536]{0:T(1024)} %param.26) | copy-start | bytes 18436
  78.3 1.5 copy-start
  78.3 145.1 %all-gather.5.cloned.1.call-start = ((), (), s32[]{:S(2)}) async-start(), calls=%async_computation.7 | async-start | bytes 10616832 | tf_op jit(solution)/shard_map/all_gather | solution.py:869
  113.8 5.1 copy-start.13
  113.8 5.6 copy-start.14
  113.8 6.2 copy-start.15
  113.8 6.8 %copy-start.16 = (f32[768]{0:T(1024)S(1)}, f32[768]{0:T(1024)}, u32[]{:S(2)}) copy-start(f32[768]{0:T(1024)} %param.34) | copy-start | bytes 9220
  113.8 7.4 %copy-start.17 = (f32[768]{0:T(1024)S(1)}, f32[768]{0:T(1024)}, u32[]{:S(2)}) copy-start(f32[768]{0:T(1024)} %param.35) | copy-start | bytes 9220
  113.9 7.9 %copy-start.18 = (f32[768]{0:T(1024)S(1)}, f32[768]{0:T(1024)}, u32[]{:S(2)}) copy-start(f32[768]{0:T(1024)} %param.36) | copy-start | bytes 9220
  113.9 8.5 %copy-start.19 = (f32[768]{0:T(1024)S(1)}, f32[768]{0:T(1024)}, u32[]{:S(2)}) copy-start(f32[768]{0:T(1024)} %param.40) | copy-start | bytes 9220
  113.9 9.1 %copy-start.11 = (f32[1536]{0:T(1024)S(1)}, f32[1536]{0:T(1024)}, u32[]{:S(2)}) copy-start(f32[1536]{0:T(1024)} %param.32) | copy-start | bytes 18436
  113.9 61.4 %all-to-all-start.1 = ((bf16[4,2,208,768]{3,2,1,0:T(8,128)(2,1)}), bf16[4,2,208,768]{3,2,1,0:T(8,128)(2,1)S(1)}, u32[]{:S(2)}, u32[]{:S(2)}) async-start(bf16[4,2,208,768]{3,2,1,0:T(8,128)(2,1)} %bitcast.72), calls=%async_computation.1 | async-start | bytes 5111808 | tf_op jit(solution)/shard_map/all_to_all | solution.py:858
  117.7 393.3 %reduce-scatter.3.cloned.1.call-start = ((), (), s32[]{:S(2)}) async-start(), calls=%async_computation.8 | async-start | bytes 10616832 | tf_op jit(solution)/shard_map/reduce_scatter | solution.py:883
  175.3 1.5 copy-start.1
  296.8 1.7 copy-start.2
  377.2 94.5 %all-to-all-start.2 = ((bf16[4,2,208,768]{3,2,1,0:T(8,128)(2,1)}), bf16[4,2,208,768]{3,2,1,0:T(8,128)(2,1)S(1)}, u32[]{:S(2)}, u32[]{:S(2)}) async-start(bf16[4,2,208,768]{3,2,1,0:T(8,128)(2,1)} %get-tuple-element.75), calls=%async_computation.2 | async-start | bytes 5111808 | tf_op jit(solution)/shard_map/all_to_all | solution.py:858
  381.1 84.5 %copy-start.12 = (f32[8,768]{1,0:T(8,128)S(1)}, f32[8,768]{1,0:T(8,128)}, u32[]{:S(2)}) copy-start(f32[8,768]{1,0:T(8,128)} %get-tuple-element.82) | copy-start | bytes 73732
  381.1 84.5 %copy-start.8 = (f32[4,8,768]{2,1,0:T(8,128)S(1)}, f32[4,8,768]{2,1,0:T(8,128)}, u32[]{:S(2)}) copy-start(f32[4,8,768]{2,1,0:T(8,128)} %get-tuple-element.81) | copy-start | bytes 294916
  471.7 1.5 copy-start.4
  506.1 3.8 copy-start.9
  506.1 128.7 %all-to-all-start.3 = ((bf16[4,2,208,768]{3,2,1,0:T(8,128)(2,1)}), bf16[4,2,208,768]{3,2,1,0:T(8,128)(2,1)S(1)}, u32[]{:S(2)}, u32[]{:S(2)}) async-start(bf16[4,2,208,768]{3,2,1,0:T(8,128)(2,1)} %bitcast.71), calls=%async_computation.3 | async-start | bytes 5111808 | tf_op jit(solution)/shard_map/all_to_all | solution.py:858
  509.9 133.5 %reduce-scatter.5.cloned.1.call-start = ((), (), s32[]{:S(2)}) async-start(), calls=%async_computation.9 | async-start | bytes 1474560 | tf_op jit(solution)/shard_map/reduce_scatter | solution.py:884
  626.1 2.4 copy-start.5
  626.1 2.7 copy-start.6
  626.1 3.0 copy-start.7
  634.8 1.5 copy-start.3
Sparse Core Ops, SparseCore 0:
  78.4 32.9 all-gather.2
  113.9 57.7 all-gather.4
  297.0 73.6 reduce-scatter.2
  512.7 54.0 reduce-scatter.4
